TPU v7x, 512 devices: a whole 4x4x16 slice. The times are simulated.
512 devices in a mesh: span: 64 (over y_hi, z, core), seq: 8 (over x, y_lo).
Axes of the slice: x: 4, y: 4 (y_hi: 2, y_lo: 2; y = y_hi * 2 + y_lo), z: 16, core: 2. Of those that a mesh axis runs over, the one named last changes fastest.
Arguments:
- queries: bfloat16 [64, 128, 3072], P('span', 'seq'), may hold values from -16 to 16
- key_value_pairs: bfloat16 [64, 128, 2048], P('span', 'seq'), may hold values from -16 to 16
- span_index: int32 [64], P('span'), may hold values from 0 to 63, each once
- valid_count: int32 [64], P('span'), may hold values from 32 to 128, as said below
Outputs:
- attended: bfloat16 [64, 128, 3072], P('span', 'seq')
Inputs may be any that keep to these rules, and one draw needn't show every extreme that they name: `span_index`: a permutation of 0 to 63. `valid_count`: some span has all 128 slots valid.
All inputs are finite; a program needn't handle non-finite values.
Results may differ from a plain program's by a relative error of at most 0.035.
Values may be sent and summed in bfloat16 or wider, within the bound.
A program may use at most 128 MiB of HBM per device.

v0:
```python
import jax
import jax.numpy as jnp
from jax import lax
from jax.sharding import PartitionSpec as P

QUERY_HEAD_COUNT = 24
KEY_VALUE_GROUPS = 8
HEAD_SIZE = 128


NEG = -1e30


def slot_mask(index_piece, valid_piece, own_index, positions):
    later = index_piece <= own_index
    return (later[:, None] & (positions[None, :] < valid_piece[:, None])).reshape(-1)


def block_update(state_now, query_head_groups, key_rows, value_rows, visible):
    row_max, row_total, weighted = state_now
    score_scale = HEAD_SIZE ** (-0.5)
    scores = (
        jnp.einsum(
            "tkgd,ukd->kgtu", query_head_groups, key_rows, preferred_element_type=jnp.float32
        )
        * score_scale
    )
    scores = jnp.where(visible, scores, NEG)
    new_max = jnp.maximum(row_max, jnp.max(scores, axis=-1))
    raw = jnp.where(visible, jnp.exp(scores - new_max[..., None]), 0.0)
    new_total = jnp.sum(raw, axis=-1)
    product = jnp.einsum(
        "kgtu,ukd->kgtd", raw.astype(jnp.bfloat16), value_rows, preferred_element_type=jnp.float32
    )
    return (new_max, new_total, product)


def guarded_update(state_now, query_head_groups, key_rows, value_rows, visible):
    return block_update(state_now, query_head_groups, key_rows, value_rows, visible)


def empty_state(kv_heads, group_list, rows):
    return (
        jnp.full((kv_heads, group_list, rows), NEG, jnp.float32),
        jnp.zeros((kv_heads, group_list, rows), jnp.float32),
        jnp.zeros((kv_heads, group_list, rows, HEAD_SIZE), jnp.float32),
    )


def shards(queries, key_value_pairs, span_index, valid_count):
    tok_dev = queries.shape[1]
    total_rows = tok_dev * lax.axis_size("seq")
    group_list = QUERY_HEAD_COUNT // KEY_VALUE_GROUPS
    own_index = span_index[0]
    query_heads, kv_heads = (
        lax.all_to_all(queries, "seq", split_axis=2, concat_axis=1, tiled=True),
        lax.all_to_all(key_value_pairs, "seq", split_axis=2, concat_axis=1, tiled=True),
    )
    local_groups = kv_heads.shape[2] // (2 * HEAD_SIZE)
    query_head_groups = query_heads.reshape(total_rows, local_groups, group_list, HEAD_SIZE)
    positions = jnp.arange(total_rows, dtype=jnp.int32)
    kv_piece = lax.all_gather(kv_heads, "span", axis=0, tiled=True)
    index_piece = lax.all_gather(span_index, "span", axis=0, tiled=True)
    valid_piece = lax.all_gather(valid_count, "span", axis=0, tiled=True)
    piece_count = kv_piece.shape[0]
    kv_split = kv_piece.reshape(piece_count * total_rows, local_groups, 2, HEAD_SIZE)
    visible = slot_mask(index_piece, valid_piece, own_index, positions)
    row_max, row_total, weighted = guarded_update(
        empty_state(local_groups, group_list, total_rows),
        query_head_groups,
        kv_split[:, :, 0],
        kv_split[:, :, 1],
        visible,
    )
    attention_output = (weighted / row_total[..., None]).astype(jnp.bfloat16)
    attention_output = attention_output.transpose(2, 0, 1, 3).reshape(
        1, total_rows, local_groups * group_list * HEAD_SIZE
    )
    return lax.all_to_all(attention_output, "seq", split_axis=1, concat_axis=2, tiled=True)


def solution(mesh):
    return jax.shard_map(
        shards,
        mesh=mesh,
        in_specs=(P("span", "seq", None), P("span", "seq", None), P("span"), P("span")),
        out_specs=P("span", "seq", None),
        check_vma=False,
    )
```

profile of v0, /device:TPU:1, one launch (start us, length us, event | category | flops | bytes accessed | tf_op | source)
XLA Modules:
  0.0 246.0 jit_solution(16246633220731027890)
XLA Ops:
  6.5 0.0 all-gather.2.cloned.1.call-start
  6.5 2.0 copy.33
  8.5 0.5 broadcast.24
  9.0 11.5 %reduce.3 = bf16[2048,16]{1,0:T(8,128)(2,1)S(1)} reduce(bf16[2048,1,16]{2,1,0:T(2,128)(2,1)S(1)} %bitcast.85, bf16[]{:T(256)} %broadcast.24), dimensions={1}, to_apply=%bitcast.72.reduce_sub_computation | reduce | bytes 131074
  20.5 0.5 reshape.70
  21.1 10.8 %all_to_all.51 = bf16[8,2,2048]{2,1,0:T(2,128)(2,1)S(1)} all-to-all(bf16[8,2,2048]{2,1,0:T(2,128)(2,1)S(1)} %reshape.70), channel_id=1, replica_groups=mesh['span'=64,'seq'=8] {'seq'}, dimensions={0} | all-to-all | bytes 131072 | tf_op jit(solution)/shard_map/all_to_all | solution.py:57
  31.9 0.9 reshape.71
  32.8 0.5 copy.34
  33.3 0.6 copy.35
  34.0 0.0 all-gather.2.cloned.1.call-update
  34.0 3.1 %copy.38 = bf16[1,16,3072]{1,0,2:T(2,128)(2,1)S(1)} copy(bf16[1,16,3072]{2,1,0:T(8,128)(2,1)} %param.4) | data formatting | bytes 196608 | tf_op args[0]
  37.1 16.9 %reduce.2 = bf16[3072,16]{1,0:T(8,128)(2,1)S(1)} reduce(bf16[3072,1,16]{2,1,0:T(2,128)(2,1)S(1)} %bitcast.84, bf16[]{:T(256)} %broadcast.24), dimensions={1}, to_apply=%bitcast.74.reduce_sub_computation | reduce | bytes 196610
  54.1 1.5 reshape.72
  55.5 3.4 %all-to-all-start.1 = ((bf16[8,2,3072]{2,1,0:T(2,128)(2,1)}), bf16[8,2,3072]{2,1,0:T(2,128)(2,1)S(1)}, u32[]{:S(2)}, u32[]{:S(2)}) async-start(bf16[8,2,3072]{2,1,0:T(2,128)(2,1)} %reshape.72), calls=%async_computation.1 | async-start | bytes 196608 | tf_op jit(solution)/shard_map/all_to_all | solution.py:56
  60.2 1.3 dynamic-slice
  61.5 0.8 dynamic-update-slice.1
  62.3 0.8 dynamic-update-slice
  63.1 28.7 %all-reduce.2 = (s32[64]{0:T(128)S(1)}, s32[64]{0:T(128)S(1)}) all-reduce(s32[64]{0:T(128)S(1)} %dynamic-update-slice.1, s32[64]{0:T(128)S(1)} %dynamic-update-slice), channel_id=1, replica_groups=mesh['span'=64,'seq'=8] {'span'}, use_global_device_ids=true, to_apply=%add.1 | all-reduce | flops 128 | bytes 1024
  91.8 0.1 fusion.23
  91.9 0.0 all-to-all-done.1
  91.9 1.2 reshape.73
  93.2 1.3 copy.39
  94.6 95.1 %all-gather.2.cloned.1.call-done = bf16[64,128,256]{2,1,0:T(8,128)(2,1)} async-done(((bf16[1,128,256]{2,1,0:T(8,128)(2,1)}), bf16[64,128,256]{2,1,0:T(8,128)(2,1)}) %all-gather.2.cloned.1.call-update) | async-done | bytes 4194320 | tf_op jit(solution)/shard_map/all_gather | solution.py:62
  189.7 6.9 %reshape.69 = bf16[8192,1,2,128]{3,2,0,1:T(2,128)(2,1)} reshape(bf16[64,128,256]{2,1,0:T(8,128)(2,1)} %all-gather.2.cloned.1.call-done) | data formatting | bytes 8388608 | tf_op jit(solution)/shard_map/reshape | solution.py:66
  196.6 9.8 %fusion.25 = (bf16[8192,1,1,128]{3,2,0,1:T(2,128)(2,1)}, bf16[8192,1,1,128]{3,2,0,1:T(2,128)(2,1)}) fusion(bf16[8192,1,2,128]{3,2,0,1:T(2,128)(2,1)} %reshape.69), kind=kLoop, calls=%fused_computation.25 | loop fusion | bytes 8388608 | tf_op jit(solution)/shard_map/slice | solution.py:72
  206.4 8.3 %copy.49 = bf16[8192,1,1,128]{0,3,2,1:T(8,128)(2,1)S(1)} copy(bf16[8192,1,1,128]{3,2,0,1:T(2,128)(2,1)} %get-tuple-element.7) | data formatting | bytes 4194304
  214.8 6.5 %bitcast_reduce_fusion = (f32[3,128]{1,0:T(4,128)S(1)}, f32[1,8192,128,3]{2,1,3,0:T(8,128)S(1)}) fusion(bf16[128,3,128]{2,1,0:T(4,128)(2,1)S(1)} %reshape.53, bf16[8192,1,1,128]{3,2,0,1:T(2,128)(2,1)} %get-tuple-element.8, pred[8192]{0:T(1024)(128)(4,1)S(1)} %fusion.23), kind=kOutput, calls=%fused_computation.1 | convolution fusion | flops 814743168 | bytes 14788096 | tf_op jit(solution)/shard_map/tkgd,ukd->kgtu/dot_general | solution.py:23
  221.2 4.4 %fusion.2 = f32[3,128]{1,0:T(4,128)S(1)} fusion(f32[1,8192,128,3]{2,1,3,0:T(8,128)S(1)} %get-tuple-element.10, f32[3,128]{1,0:T(4,128)S(1)} %broadcast_maximum_fusion, pred[8192]{0:T(1024)(128)(4,1)S(1)} %fusion.23), kind=kLoop, calls=%fused_computation.5 | loop fusion | flops 9436800 | bytes 12594176 | tf_op jit(solution)/shard_map/reduce_sum | solution.py:31
  225.7 2.4 fusion.16
  228.0 0.2 copy.43
  228.2 1.2 reduce.4
  229.4 9.0 %all_to_all.52 = bf16[8,2,3072]{2,1,0:T(2,128)(2,1)S(1)} all-to-all(bf16[8,2,3072]{2,1,0:T(2,128)(2,1)S(1)} %reshape.74), channel_id=1, replica_groups=mesh['span'=64,'seq'=8] {'seq'}, dimensions={0} | all-to-all | bytes 196608 | tf_op jit(solution)/shard_map/all_to_all | solution.py:79
  238.4 0.1 reshape.75
  238.5 0.7 copy.51
  (12 shorter events, 0.2 us)
Async XLA Ops:
  6.5 183.2 %all-gather.2.cloned.1.call-start = ((), (), s32[]{:S(2)}) async-start(), calls=%async_computation.3 | async-start | bytes 4259840 | tf_op jit(solution)/shard_map/all_gather | solution.py:62
  55.5 36.4 %all-to-all-start.1 = ((bf16[8,2,3072]{2,1,0:T(2,128)(2,1)}), bf16[8,2,3072]{2,1,0:T(2,128)(2,1)S(1)}, u32[]{:S(2)}, u32[]{:S(2)}) async-start(bf16[8,2,3072]{2,1,0:T(2,128)(2,1)} %reshape.72), calls=%async_computation.1 | async-start | bytes 196608 | tf_op jit(solution)/shard_map/all_to_all | solution.py:56
Sparse Core Ops, SparseCore 0:
  34.1 155.5 all-gather.1
where the time goes:
time: 247 us; the launch traced here: 246 us
  waiting for transfers between devices  95.1 us (39%)
  blocking collectives  48.5 us (20%)
  local copies, waits for them, and re-layouts  41.2 us (17%)
  other arithmetic  34.1 us (14%)
  between operations  14.9 us (6%)
  matrix products  8.83 us (4%)
  starting transfers between devices  3.36 us (1%)
    all_gather x1, waiting for transfers between devices, shards(): kv_piece = lax.all_gather(kv_heads, 'span', axis=0, tiled=True)  95.1 us
    unnamed x3, other arithmetic  29.6 us
    unnamed x1, blocking collectives  28.7 us
    unnamed x18, local copies, waits for them, and re-layouts  21.2 us
    all_to_all x1, blocking collectives, shards(): lax.all_to_all(key_value_pairs, 'seq', split_axis=2, concat_axis=1, tiled...  10.8 us
    slice x1, local copies, waits for them, and re-layouts, shards(): kv_split[:, :, 1]  9.8 us
    all_to_all x1, blocking collectives, shards(): lax.all_to_all(attention_output, 'seq', split_axis=1, concat_axis=2, tile...  8.98 us
    reshape x1, local copies, waits for them, and re-layouts, shards(): kv_piece.reshape(piece_count * total_rows, local_groups, 2, HEAD_SIZE)  6.92 us
  transfers between devices with their start and end apart: 2, of which 1 were waited for; matrix products, arithmetic and copies ran while one was open for 11% of the time, Pallas kernels for 0%

commit v1 on v0

v1 whole, which is shorter than its diff:
```python
import functools
import math

import jax
import jax.numpy as jnp
from jax import lax
from jax.experimental import pallas as pl
from jax.experimental.pallas import tpu as pltpu
from jax.sharding import PartitionSpec as P

MESH = pl.DeviceIdType.MESH
HEAD = 128
LIST = 3
KEYS = 128
META = 16
ROW_EXTRA = 128
SCALE = HEAD ** (-0.5) / math.log(2.0)
NO_MAX = -(2.0**100)
HIDDEN = -(2.0**101)
FAR = 100.0


def kernel(
    n_span, n_seq,
    q_hbm, kv_hbm, index_ref, count_ref, out_ref,
    kbuf, vbuf, qbuf, own_meta, partner_meta, max_ref, sum_ref, acc_ref, part_buf, got_buf,
    a2a_send, a2a_recv, ring_send, k_recv, v_recv,
):
    tokens = q_hbm.shape[1]
    half_spans = n_span // 2
    n_z = half_spans // 2
    span = lax.axis_index("span")
    seq = lax.axis_index("seq")
    half = lax.div(span, half_spans)
    slot = lax.rem(span, half_spans)
    z = lax.div(slot, 2)
    core = lax.rem(slot, 2)
    group = seq ^ half
    partner_span = (1 - half) * half_spans + slot
    sibling = (half * half_spans + z * 2 + (1 - core), seq)

    def z_at(offset):
        return lax.rem(z + offset + n_z, n_z)

    up = (half * half_spans + z_at(1) * 2 + core, seq)
    down = (half * half_spans + z_at(-1) * 2 + core, seq)

    barrier = pltpu.get_barrier_semaphore()
    for d in range(1, n_seq):
        pl.semaphore_signal(barrier, inc=1, device_id=(span, seq ^ d), device_id_type=MESH)
    for d in range(n_seq):
        pl.semaphore_signal(barrier, inc=1, device_id=(partner_span, seq ^ d), device_id_type=MESH)
    for device in (up, down, sibling):
        pl.semaphore_signal(barrier, inc=1, device_id=device, device_id_type=MESH)
    pl.semaphore_wait(barrier, 2 * n_seq + 2)

    def send(src, dst, send_sem, recv_sem, device):
        pltpu.make_async_remote_copy(
            src_ref=src, dst_ref=dst, send_sem=send_sem, recv_sem=recv_sem, device_id=device, device_id_type=MESH
        ).start()

    def wait(ref, sem):
        pltpu.make_async_copy(ref, ref, sem).wait()

    rows = pl.ds(pl.multiple_of(seq * tokens, tokens), tokens)

    def columns(start, size):
        return pl.ds(pl.multiple_of(start, 128), size)

    for part, buf in ((0, kbuf), (1, vbuf)):
        for d in range(n_seq):
            their = (seq ^ d) ^ half
            src = kv_hbm.at[0, :, columns(their * 256 + part * 128, 128)]
            dst = buf.at[slot, rows, :]
            if d == 0:
                pltpu.make_async_copy(src, dst, a2a_recv.at[part]).start()
            else:
                send(src, dst, a2a_send.at[part], a2a_recv.at[part], (span, seq ^ d))

    for d in range(n_seq):
        their = (seq ^ d) ^ half
        src = q_hbm.at[0, :, columns(their * (LIST * HEAD), LIST * HEAD)]
        dst = qbuf.at[0, rows, :]
        if d == 0:
            pltpu.make_async_copy(src, dst, a2a_recv.at[2]).start()
        else:
            send(src, dst, a2a_send.at[2], a2a_recv.at[2], (span, seq ^ d))
    for d in range(n_seq):
        their = (seq ^ d) ^ (1 - half)
        src = q_hbm.at[0, :, columns(their * (LIST * HEAD), LIST * HEAD)]
        send(src, qbuf.at[1, rows, :], a2a_send.at[3], a2a_recv.at[3], (partner_span, seq ^ d))

    index = index_ref[0].astype(jnp.float32)
    count = count_ref[0]
    lane = lax.broadcasted_iota(jnp.int32, (META, 128), 1)
    kbuf[slot, KEYS:, :] = jnp.where(lane < count, index, FAR).astype(jnp.bfloat16)
    own_meta[...] = jnp.full((META, 128), index, jnp.float32).astype(jnp.bfloat16)
    send(own_meta, partner_meta, a2a_send.at[4], a2a_recv.at[4], (partner_span, seq ^ 1))

    max_ref[...] = jnp.full(max_ref.shape, NO_MAX, jnp.float32)
    sum_ref[...] = jnp.zeros(sum_ref.shape, jnp.float32)
    acc_ref[...] = jnp.zeros(acc_ref.shape, jnp.float32)

    def pass_on(buf, recv, send_sem, which, device):
        send(buf.at[which], buf.at[which], send_sem, recv.at[which], device)

    def pass_k(which, device):
        pass_on(kbuf, k_recv, ring_send.at[0], which, device)

    def pass_v(which, device):
        pass_on(vbuf, v_recv, ring_send.at[1], which, device)

    def wait_k(which):
        wait(kbuf.at[which], k_recv.at[which])

    def wait_v(which):
        wait(vbuf.at[which], v_recv.at[which])

    wait(kbuf.at[slot, pl.ds(0, KEYS), :], a2a_recv.at[0])
    for device in (up, down, sibling):
        pass_k(slot, device)
    wait(vbuf.at[slot], a2a_recv.at[1])
    for device in (up, down, sibling):
        pass_v(slot, device)

    def update(b, head, places):
        tile = b * LIST + head
        query = qbuf[b, :, head * HEAD : (head + 1) * HEAD]
        if b == 0:
            mine = own_meta[...].astype(jnp.float32)[:1]
        else:
            mine = partner_meta[...].astype(jnp.float32)[:1]
        scores = []
        for place in places:
            pair = pl.ds(place * 2, 2)
            keys = kbuf[pair, :KEYS, :].reshape(2 * KEYS, HEAD)
            meta = kbuf[pair, KEYS:, :].astype(jnp.float32)
            product = lax.dot_general(
                query, keys, (((1,), (1,)), ((), ())), preferred_element_type=jnp.float32
            )
            for i in range(2):
                bias = jnp.where(meta[i, :1] <= mine, 0.0, HIDDEN)
                scores.append(product[:, i * KEYS : (i + 1) * KEYS] * SCALE + bias)
        top = functools.reduce(jnp.maximum, scores)
        old_max = max_ref[tile]
        new_max = jnp.maximum(old_max, jnp.max(top, axis=-1, keepdims=True))
        alpha = jnp.exp2(old_max - new_max)
        raw = [jnp.exp2(s - new_max) for s in scores]
        max_ref[tile] = new_max
        sum_ref[tile] = sum_ref[tile] * alpha + functools.reduce(jnp.add, raw)
        total = acc_ref[tile] * alpha
        for i, place in enumerate(places):
            values = vbuf[pl.ds(place * 2, 2)].reshape(2 * KEYS, HEAD)
            weights = jnp.concatenate(raw[2 * i : 2 * i + 2], axis=1).astype(jnp.bfloat16)
            total += jnp.dot(weights, values, preferred_element_type=jnp.float32)
        acc_ref[tile] = total

    def wait_other(place):
        wait_k(place * 2 + 1 - core)
        wait_v(place * 2 + 1 - core)

    def own(place):
        return place * 2 + core

    def step(h, places, first=False):
        def tiles(*which):
            for i in which:
                update(i // LIST, i % LIST, places)

        before, after = own(z_at(-h)), own(z_at(h))
        wait_k(before)
        pass_k(before, up)
        pass_k(before, sibling)
        if first:
            wait(qbuf.at[0], a2a_recv.at[2])
            wait(qbuf.at[1], a2a_recv.at[3])
            wait(partner_meta, a2a_recv.at[4])
        for place in places:
            wait_other(place)
        tiles(0, 1)
        wait_k(after)
        pl.when(h < n_z // 2 - 1)(lambda: pass_k(after, down))
        pass_k(after, sibling)
        tiles(2)
        wait_v(before)
        pl.when(h < n_z // 2 - 1)(lambda: pass_v(before, up))
        pass_v(before, sibling)
        tiles(3, 4)
        wait_v(after)
        pass_v(after, down)
        pass_v(after, sibling)
        tiles(5)

    step(1, [z], first=True)

    def loop(h, carry):
        step(h, [z_at(1 - h), z_at(h - 1)])
        return carry

    lax.fori_loop(2, n_z // 2, loop, 0)

    last = z_at(n_z // 2)
    places = [z_at(1 - n_z // 2), z_at(n_z // 2 - 1)]
    wait_k(own(last))
    pass_k(own(last), sibling)
    for place in places:
        wait_other(place)
    for i in range(3):
        update(i // LIST, i % LIST, places)
    wait_v(own(last))
    pass_v(own(last), sibling)
    for i in range(3, 6):
        update(i // LIST, i % LIST, places)
    wait_other(last)
    lane = lax.broadcasted_iota(jnp.int32, (KEYS, 128), 1)
    for b in (1, 0):
        stats = jnp.zeros((KEYS, 128), jnp.float32)
        for head in range(LIST):
            update(b, head, [last])
            tile = b * LIST + head
            top = max_ref[tile]
            sent_max = top.astype(jnp.bfloat16).astype(jnp.float32)
            factor = jnp.exp2(top - sent_max)
            total = jnp.sum(sum_ref[tile], axis=-1, keepdims=True) * factor
            high = total.astype(jnp.bfloat16).astype(jnp.float32)
            stats = jnp.where(lane == 3 * head, sent_max, stats)
            stats = jnp.where(lane == 3 * head + 1, high, stats)
            stats = jnp.where(lane == 3 * head + 2, total - high, stats)
            part_buf[b, :, head * HEAD : (head + 1) * HEAD] = (acc_ref[tile] * factor).astype(jnp.bfloat16)
        part_buf[b, :, LIST * HEAD :] = stats.astype(jnp.bfloat16)
        for d in range(n_seq):
            to = seq ^ d
            src = part_buf.at[b, pl.ds(pl.multiple_of(to * tokens, tokens), tokens), :]
            dst = got_buf.at[b, group]
            if b == 0 and d == 0:
                pltpu.make_async_copy(src, dst, a2a_recv.at[5]).start()
            else:
                device = (span if b == 0 else partner_span, to)
                send(src, dst, a2a_send.at[5 + b], a2a_recv.at[5 + b], device)

    wait(kbuf.at[pl.ds(0, half_spans - 1)], ring_send.at[0])
    wait(vbuf.at[pl.ds(0, half_spans - 1)], ring_send.at[1])
    wait(vbuf.at[0, pl.ds(0, (n_seq - 1) * tokens), :], a2a_send.at[0])
    wait(vbuf.at[0, pl.ds(0, (n_seq - 1) * tokens), :], a2a_send.at[1])
    wait(qbuf.at[0, pl.ds(0, (n_seq - 1) * tokens), :], a2a_send.at[2])
    wait(qbuf.at[1], a2a_send.at[3])
    wait(own_meta, a2a_send.at[4])

    wait(got_buf.at[1], a2a_recv.at[6])
    wait(got_buf.at[0], a2a_recv.at[5])
    for g in range(n_seq):
        stats = [got_buf[b, g, :, LIST * HEAD :].astype(jnp.float32) for b in range(2)]
        for head in range(LIST):
            tops = [s[:, 3 * head : 3 * head + 1] for s in stats]
            totals = [s[:, 3 * head + 1 : 3 * head + 2] + s[:, 3 * head + 2 : 3 * head + 3] for s in stats]
            top = jnp.maximum(*tops)
            shares = [jnp.exp2(t - top) for t in tops]
            whole = shares[0] * totals[0] + shares[1] * totals[1]
            shares = [s / whole for s in shares]
            parts = [got_buf[b, g, :, head * HEAD : (head + 1) * HEAD].astype(jnp.float32) for b in range(2)]
            place = (g * LIST + head) * HEAD
            out_ref[0, :, place : place + HEAD] = (parts[0] * shares[0] + parts[1] * shares[1]).astype(jnp.bfloat16)
    wait(part_buf.at[0, pl.ds(0, (n_seq - 1) * tokens), :], a2a_send.at[5])
    wait(part_buf.at[1], a2a_send.at[6])


def solution(mesh):
    n_span, n_seq = mesh.shape["span"], mesh.shape["seq"]
    slots = n_span // 2

    def shards(queries, key_value_pairs, span_index, valid_count):
        tokens = queries.shape[1]
        return pl.pallas_call(
            functools.partial(kernel, n_span, n_seq),
            out_shape=jax.ShapeDtypeStruct(queries.shape, jnp.bfloat16),
            in_specs=[pl.BlockSpec(memory_space=pl.ANY)] * 2 + [pl.BlockSpec(memory_space=pltpu.SMEM)] * 2,
            out_specs=pl.BlockSpec(memory_space=pltpu.VMEM),
            scratch_shapes=[
                pltpu.VMEM((slots, KEYS + META, HEAD), jnp.bfloat16),
                pltpu.VMEM((slots, KEYS, HEAD), jnp.bfloat16),
                pltpu.VMEM((2, KEYS, LIST * HEAD), jnp.bfloat16),
                pltpu.VMEM((META, 128), jnp.bfloat16),
                pltpu.VMEM((META, 128), jnp.bfloat16),
                pltpu.VMEM((2 * LIST, KEYS, HEAD), jnp.float32),
                pltpu.VMEM((2 * LIST, KEYS, HEAD), jnp.float32),
                pltpu.VMEM((2 * LIST, KEYS, HEAD), jnp.float32),
                pltpu.VMEM((2, KEYS, LIST * HEAD + ROW_EXTRA), jnp.bfloat16),
                pltpu.VMEM((2, n_seq, tokens, LIST * HEAD + ROW_EXTRA), jnp.bfloat16),
                pltpu.SemaphoreType.DMA((7,)),
                pltpu.SemaphoreType.DMA((7,)),
                pltpu.SemaphoreType.DMA((2,)),
                pltpu.SemaphoreType.DMA((slots,)),
                pltpu.SemaphoreType.DMA((slots,)),
            ],
            compiler_params=pltpu.CompilerParams(
                collective_id=0, has_side_effects=True, vmem_limit_bytes=32 * 1024 * 1024
            ),
        )(queries, key_value_pairs, span_index, valid_count)

    return jax.shard_map(
        shards,
        mesh=mesh,
        in_specs=(P("span", "seq", None), P("span", "seq", None), P("span"), P("span")),
        out_specs=P("span", "seq", None),
        check_vma=False,
    )
```

time: 247 us -> 60.1 us (0.24)
  waiting for transfers between devices: 95.1 us -> 0 us
  Pallas kernels: 0 us -> 56.2 us
  blocking collectives: 48.5 us -> 0 us
  local copies, waits for them, and re-layouts: 41.2 us -> 2.37 us
  other arithmetic: 34.1 us -> 0 us
  between operations: 14.9 us -> 1.31 us
  matrix products: 8.83 us -> 0 us
  starting transfers between devices: 3.36 us -> 0 us
    all_gather x1 -> x0, waiting for transfers between devices: 95.1 us -> none  [shards(): kv_piece = lax.all_gather(kv_heads, 'span', axis=0, tiled=True)]
    pallas_call x0 -> x1, Pallas kernels: none -> 56.2 us  [shards(): pl.pallas_call(functools.partial(kernel, n_span, n_seq), out_shape=jax.Sh...]
    unnamed x3 -> x0, other arithmetic: 29.6 us -> none
    unnamed x1 -> x0, blocking collectives: 28.7 us -> none
    all_to_all x2 -> x0, blocking collectives: 19.7 us -> none  [the longest x1 10.8 us: shards(): lax.all_to_all(key_value_pairs, 'seq', split_axis=2, concat_axis=1, tiled...]
    unnamed x18 -> x5, local copies, waits for them, and re-layouts: 21.2 us -> 2.37 us
    slice x1 -> x0, local copies, waits for them, and re-layouts: 9.8 us -> none  [shards(): kv_split[:, :, 1]]
    dot_general x2 -> x0, matrix products: 8.83 us -> none  [the longest x1 6.46 us: block_update(): jnp.einsum('tkgd,ukd->kgtu', query_head_groups, key_rows, preferred_eleme...]
  transfers between devices with their start and end apart: 2 -> 0, of which waited for: 1 -> 0; matrix products, arithmetic and copies ran while one was open for 11% -> 0% of each run, Pallas kernels for 0% -> 0%
where the time goes in v1:
time: 60.1 us; the launch traced here: 59.9 us
  Pallas kernels  56.2 us (94%)
  local copies, waits for them, and re-layouts  2.37 us (4%)
  between operations  1.31 us (2%)
    pallas_call x1, Pallas kernels, shards(): pl.pallas_call(functools.partial(kernel, n_span, n_seq), out_shape=jax.Sh...  56.2 us
    unnamed x5, local copies, waits for them, and re-layouts  2.37 us

profile of v1, /device:TPU:1, one launch (start us, length us, event | category | flops | bytes accessed | tf_op | source)
XLA Modules:
  0.0 59.9 jit_solution(17147282344586409468)
XLA Ops:
  1.3 0.0 copy-start
  1.3 0.9 %copy-done = bf16[1,16,3072]{2,1,0:T(8,128)(2,1)S(1)} copy-done((bf16[1,16,3072]{2,1,0:T(8,128)(2,1)S(1)}, bf16[1,16,3072]{2,1,0:T(8,128)(2,1)}, u32[]{:S(2)}) %copy-start) | copy-done | bytes 98328
  2.2 0.0 copy-start.1
  2.2 0.8 %copy-done.1 = bf16[1,16,2048]{2,1,0:T(8,128)(2,1)S(1)} copy-done((bf16[1,16,2048]{2,1,0:T(8,128)(2,1)S(1)}, bf16[1,16,2048]{2,1,0:T(8,128)(2,1)}, u32[]{:S(2)}) %copy-start.1) | copy-done | bytes 65560
  3.0 56.2 %shard_map.46 = bf16[1,16,3072]{2,1,0:T(8,128)(2,1)S(1)} custom-call(bf16[1,16,3072]{2,1,0:T(8,128)(2,1)S(1)} %copy-done, bf16[1,16,2048]{2,1,0:T(8,128)(2,1)S(1)} %copy-done.1, s32[1]{0:T(128)S(6)} %copy.6.index_ref, s32[1]{0:T(128)S(6)} %copy.7.count_ref), custom_call_target="tpu_custom_call" | custom-call | tf_op jit(solution)/shard_map/pallas_call | solution.py:273
  59.3 0.6 %copy.8 = bf16[1,16,3072]{2,1,0:T(8,128)(2,1)} copy(bf16[1,16,3072]{2,1,0:T(8,128)(2,1)S(1)} %shard_map.46) | data formatting | bytes 196608
Async XLA Ops:
  1.3 0.9 %copy-start = (bf16[1,16,3072]{2,1,0:T(8,128)(2,1)S(1)}, bf16[1,16,3072]{2,1,0:T(8,128)(2,1)}, u32[]{:S(2)}) copy-start(bf16[1,16,3072]{2,1,0:T(8,128)(2,1)} %q_hbm.1) | copy-start | bytes 294916
  2.2 0.8 %copy-start.1 = (bf16[1,16,2048]{2,1,0:T(8,128)(2,1)S(1)}, bf16[1,16,2048]{2,1,0:T(8,128)(2,1)}, u32[]{:S(2)}) copy-start(bf16[1,16,2048]{2,1,0:T(8,128)(2,1)} %kv_hbm.1) | copy-start | bytes 196612

commit v2 on v1

v2 whole, which is shorter than its diff:
```python
import functools
import math

import jax
import jax.numpy as jnp
from jax import lax
from jax.experimental import pallas as pl
from jax.experimental.pallas import tpu as pltpu
from jax.sharding import PartitionSpec as P

MESH = pl.DeviceIdType.MESH
HEAD = 128
LIST = 3
KEYS = 128
META = 16
ROW_EXTRA = 128
SCALE = HEAD ** (-0.5) / math.log(2.0)
NO_MAX = -(2.0**100)
HIDDEN = -(2.0**101)
FAR = 100.0


TREES = (
    {-7: -6, -6: -5, -5: -1, -4: -5, -3: -2, -2: -1, -1: 0, 1: 0, 2: 0, 3: 2, 4: 1, 5: 4, 6: 4, 7: 5, 8: -6},
    {-7: -6, -6: -4, -5: -4, -4: 0, -3: -4, -2: -3, -1: 0, 1: 2, 2: 0, 3: 0, 4: 3, 5: 4, 6: 3, 7: 6, 8: -5},
)
GROUPS = ((0, -1), (2, 3), (-5, 4), (1, -3), (-6, -4), (-2, 6), (5, -7), (8, 7))
EVENTS = (
    ((0, -1), (0, 1), (1, -1), (0, 2),),
    (),
    ((1, -4), (1, 2), (1, 3), (0, -2), (0, 4), (0, -5), (0, 3), (1, -5), (1, -3), (1, 4), (1, 1),),
    (),
    ((1, -6), (0, -3),),
    (),
    ((0, 5), (0, -6), (1, 6),),
    (),
    ((0, -4), (1, 8), (1, -2), (1, -7), (0, 6),),
    ((1, 5),),
    ((0, -7),),
    ((1, 7),),
    ((0, 8),),
    ((0, 7),),
    (),
)
CHILDREN = tuple(
    {parent: [child for child in tree if tree[child] == parent] for parent in set(tree.values())} for tree in TREES
)


def hops(child, parent):
    return (child - parent + 8) % 16 - 8


def kernel(
    n_span, n_seq,
    q_hbm, kv_hbm, index_hbm, count_hbm, out_ref,
    kbuf, vbuf, qbuf, place_buf, max_ref, sum_ref, acc_ref, part_buf, got_buf, index_smem, count_smem,
    a2a_send, a2a_recv, ring_send, k_recv, v_recv, int_sem,
):
    tokens = q_hbm.shape[1]
    half_spans = n_span // 2
    n_z = half_spans // 2
    span = lax.axis_index("span")
    seq = lax.axis_index("seq")
    half = lax.div(span, half_spans)
    slot = lax.rem(span, half_spans)
    z = lax.div(slot, 2)
    core = lax.rem(slot, 2)
    group = seq ^ half
    partner_span = (1 - half) * half_spans + slot
    sibling = (half * half_spans + z * 2 + (1 - core), seq)

    def z_at(offset):
        return lax.rem(z + offset + n_z, n_z)

    def along(offset):
        return (half * half_spans + z_at(offset) * 2 + core, seq)

    barrier = pltpu.get_barrier_semaphore()
    for d in range(1, n_seq):
        pl.semaphore_signal(barrier, inc=1, device_id=(span, seq ^ d), device_id_type=MESH)
    for d in range(n_seq):
        pl.semaphore_signal(barrier, inc=1, device_id=(partner_span, seq ^ d), device_id_type=MESH)
    steps = sorted({abs(hops(child, parent)) for tree in TREES for child, parent in tree.items()})
    for s in steps:
        for device in (along(s), along(-s)):
            pl.semaphore_signal(barrier, inc=1, device_id=device, device_id_type=MESH)
    pl.semaphore_signal(barrier, inc=1, device_id=sibling, device_id_type=MESH)

    ints = [
        pltpu.make_async_copy(index_hbm, index_smem, int_sem.at[0]),
        pltpu.make_async_copy(count_hbm, count_smem, int_sem.at[1]),
    ]
    for copy in ints:
        copy.start()
    max_ref[...] = jnp.full(max_ref.shape, NO_MAX, jnp.float32)
    sum_ref[...] = jnp.zeros(sum_ref.shape, jnp.float32)
    acc_ref[...] = jnp.zeros(acc_ref.shape, jnp.float32)
    for copy in ints:
        copy.wait()
    index = index_smem[0].astype(jnp.float32)
    lane = lax.broadcasted_iota(jnp.int32, (META, 128), 1)
    kbuf[slot, KEYS:, :] = jnp.where(lane < count_smem[0], index, FAR).astype(jnp.bfloat16)
    place_buf[0] = jnp.full((META, 128), index, jnp.float32).astype(jnp.bfloat16)

    pl.semaphore_wait(barrier, 2 * n_seq + 2 * len(steps))

    def send(src, dst, send_sem, recv_sem, device):
        pltpu.make_async_remote_copy(
            src_ref=src, dst_ref=dst, send_sem=send_sem, recv_sem=recv_sem, device_id=device, device_id_type=MESH
        ).start()

    def wait(ref, sem):
        pltpu.make_async_copy(ref, ref, sem).wait()

    rows = pl.ds(pl.multiple_of(seq * tokens, tokens), tokens)

    def columns(start, size):
        return pl.ds(pl.multiple_of(start, 128), size)

    for part, buf in ((0, kbuf), (1, vbuf)):
        for d in range(n_seq):
            their = (seq ^ d) ^ half
            src = kv_hbm.at[0, :, columns(their * 256 + part * 128, 128)]
            dst = buf.at[slot, rows, :]
            if d == 0:
                pltpu.make_async_copy(src, dst, a2a_recv.at[part]).start()
            else:
                send(src, dst, a2a_send.at[part], a2a_recv.at[part], (span, seq ^ d))

    for d in range(n_seq):
        their = (seq ^ d) ^ half
        src = q_hbm.at[0, :, columns(their * (LIST * HEAD), LIST * HEAD)]
        dst = qbuf.at[0, rows, :]
        if d == 0:
            pltpu.make_async_copy(src, dst, a2a_recv.at[2]).start()
        else:
            send(src, dst, a2a_send.at[2], a2a_recv.at[2], (span, seq ^ d))
    for d in range(n_seq):
        their = (seq ^ d) ^ (1 - half)
        src = q_hbm.at[0, :, columns(their * (LIST * HEAD), LIST * HEAD)]
        send(src, qbuf.at[1, rows, :], a2a_send.at[3], a2a_recv.at[3], (partner_span, seq ^ d))

    send(place_buf.at[0], place_buf.at[1], a2a_send.at[4], a2a_recv.at[4], (partner_span, seq ^ 1))

    bufs, recvs = (kbuf, vbuf), (k_recv, v_recv)

    def pass_on(chunk, which, device):
        send(bufs[chunk].at[which], bufs[chunk].at[which], ring_send.at[chunk], recvs[chunk].at[which], device)

    def wait_for(chunk, which):
        wait(bufs[chunk].at[which], recvs[chunk].at[which])

    def hand_on(chunk, offset):
        which = z_at(-offset) * 2 + core
        for child in CHILDREN[chunk].get(offset, ()):
            pass_on(chunk, which, along(hops(child, offset)))
        pass_on(chunk, which, sibling)

    wait(kbuf.at[slot, pl.ds(0, KEYS), :], a2a_recv.at[0])
    hand_on(0, 0)
    wait(vbuf.at[slot], a2a_recv.at[1])
    hand_on(1, 0)
    wait(qbuf.at[0], a2a_recv.at[2])
    wait(qbuf.at[1], a2a_recv.at[3])
    wait(place_buf.at[1], a2a_recv.at[4])

    def attend(b, places):
        mine = place_buf[b].astype(jnp.float32)[:1]
        pairs = [pl.ds(place * 2, 2) for place in places]
        metas = [kbuf[pair, KEYS:, :].astype(jnp.float32) for pair in pairs]
        biases = [jnp.where(meta[i, :1] <= mine, 0.0, HIDDEN) for meta in metas for i in range(2)]
        products = []
        for head in range(LIST):
            query = qbuf[b, :, head * HEAD : (head + 1) * HEAD]
            for pair in pairs:
                keys = kbuf[pair, :KEYS, :].reshape(2 * KEYS, HEAD)
                products.append(
                    lax.dot_general(query, keys, (((1,), (1,)), ((), ())), preferred_element_type=jnp.float32)
                )
        weights = []
        for head in range(LIST):
            tile = b * LIST + head
            scores = []
            for i, bias in enumerate(biases):
                product = products[head * len(pairs) + i // 2]
                scores.append(product[:, i % 2 * KEYS : (i % 2 + 1) * KEYS] * SCALE + bias)
            old_max = max_ref[tile]
            top = functools.reduce(jnp.maximum, scores)
            new_max = jnp.maximum(old_max, jnp.max(top, axis=-1, keepdims=True))
            alpha = jnp.exp2(old_max - new_max)
            raw = [jnp.exp2(score - new_max) for score in scores]
            max_ref[tile] = new_max
            sum_ref[tile] = sum_ref[tile] * alpha + functools.reduce(jnp.add, raw)
            weights.append((alpha, [w.astype(jnp.bfloat16) for w in raw]))
        for head in range(LIST):
            tile = b * LIST + head
            alpha, raw = weights[head]
            total = acc_ref[tile] * alpha
            for i, pair in enumerate(pairs):
                values = vbuf[pair].reshape(2 * KEYS, HEAD)
                total += jnp.dot(
                    jnp.concatenate(raw[2 * i : 2 * i + 2], axis=1), values, preferred_element_type=jnp.float32
                )
            acc_ref[tile] = total

    def finish(b):
        lane = lax.broadcasted_iota(jnp.int32, (KEYS, 128), 1)
        stats = jnp.zeros((KEYS, 128), jnp.float32)
        for head in range(LIST):
            tile = b * LIST + head
            top = max_ref[tile]
            sent_max = top.astype(jnp.bfloat16).astype(jnp.float32)
            factor = jnp.exp2(top - sent_max)
            total = jnp.sum(sum_ref[tile], axis=-1, keepdims=True) * factor
            high = total.astype(jnp.bfloat16).astype(jnp.float32)
            stats = jnp.where(lane == 3 * head, sent_max, stats)
            stats = jnp.where(lane == 3 * head + 1, high, stats)
            stats = jnp.where(lane == 3 * head + 2, total - high, stats)
            part_buf[b, :, head * HEAD : (head + 1) * HEAD] = (acc_ref[tile] * factor).astype(jnp.bfloat16)
        part_buf[b, :, LIST * HEAD :] = stats.astype(jnp.bfloat16)
        for d in range(n_seq):
            to = seq ^ d
            src = part_buf.at[b, pl.ds(pl.multiple_of(to * tokens, tokens), tokens), :]
            dst = got_buf.at[b, group]
            if b == 0 and d == 0:
                pltpu.make_async_copy(src, dst, a2a_recv.at[5]).start()
            else:
                device = (span if b == 0 else partner_span, to)
                send(src, dst, a2a_send.at[5 + b], a2a_recv.at[5 + b], device)

    def places_of(g):
        places = []
        for which in range(2):
            offset = GROUPS[0][which]
            for i in range(1, len(GROUPS)):
                offset = jnp.where(g == i, GROUPS[i][which], offset)
            places.append(z_at(-offset))
        return places

    def loop(i, carry):
        for at, events in enumerate(EVENTS):
            if events:

                @pl.when(i == at)
                def _():
                    for chunk, offset in events:
                        wait_for(chunk, z_at(-offset) * 2 + core)
                        hand_on(chunk, offset)

        places = places_of(lax.div(i, 2))

        @pl.when(lax.rem(i, 2) == 0)
        def _():
            for place in places:
                for chunk in range(2):
                    wait_for(chunk, place * 2 + 1 - core)

        attend(1 - lax.rem(i, 2), places)
        return carry

    lax.fori_loop(0, 2 * len(GROUPS) - 1, loop, 0)
    finish(1)
    attend(0, [z_at(-offset) for offset in GROUPS[-1]])
    finish(0)

    wait(kbuf.at[pl.ds(0, half_spans - 1)], ring_send.at[0])
    wait(vbuf.at[pl.ds(0, half_spans - 1)], ring_send.at[1])
    wait(vbuf.at[0, pl.ds(0, (n_seq - 1) * tokens), :], a2a_send.at[0])
    wait(vbuf.at[0, pl.ds(0, (n_seq - 1) * tokens), :], a2a_send.at[1])
    wait(qbuf.at[0, pl.ds(0, (n_seq - 1) * tokens), :], a2a_send.at[2])
    wait(qbuf.at[1], a2a_send.at[3])
    wait(place_buf.at[0], a2a_send.at[4])

    wait(got_buf.at[1], a2a_recv.at[6])
    wait(got_buf.at[0], a2a_recv.at[5])
    for g in range(n_seq):
        stats = [got_buf[b, g, :, LIST * HEAD :].astype(jnp.float32) for b in range(2)]
        for head in range(LIST):
            tops = [s[:, 3 * head : 3 * head + 1] for s in stats]
            totals = [s[:, 3 * head + 1 : 3 * head + 2] + s[:, 3 * head + 2 : 3 * head + 3] for s in stats]
            top = jnp.maximum(*tops)
            shares = [jnp.exp2(t - top) for t in tops]
            whole = shares[0] * totals[0] + shares[1] * totals[1]
            shares = [s / whole for s in shares]
            parts = [got_buf[b, g, :, head * HEAD : (head + 1) * HEAD].astype(jnp.float32) for b in range(2)]
            place = (g * LIST + head) * HEAD
            out_ref[0, :, place : place + HEAD] = (parts[0] * shares[0] + parts[1] * shares[1]).astype(jnp.bfloat16)
    wait(part_buf.at[0, pl.ds(0, (n_seq - 1) * tokens), :], a2a_send.at[5])
    wait(part_buf.at[1], a2a_send.at[6])


def solution(mesh):
    n_span, n_seq = mesh.shape["span"], mesh.shape["seq"]
    slots = n_span // 2

    def shards(queries, key_value_pairs, span_index, valid_count):
        tokens = queries.shape[1]
        return pl.pallas_call(
            functools.partial(kernel, n_span, n_seq),
            out_shape=jax.ShapeDtypeStruct(queries.shape, jnp.bfloat16),
            in_specs=[pl.BlockSpec(memory_space=pl.ANY)] * 4,
            out_specs=pl.BlockSpec(memory_space=pltpu.VMEM),
            scratch_shapes=[
                pltpu.VMEM((slots, KEYS + META, HEAD), jnp.bfloat16),
                pltpu.VMEM((slots, KEYS, HEAD), jnp.bfloat16),
                pltpu.VMEM((2, KEYS, LIST * HEAD), jnp.bfloat16),
                pltpu.VMEM((2, META, 128), jnp.bfloat16),
                pltpu.VMEM((2 * LIST, KEYS, HEAD), jnp.float32),
                pltpu.VMEM((2 * LIST, KEYS, HEAD), jnp.float32),
                pltpu.VMEM((2 * LIST, KEYS, HEAD), jnp.float32),
                pltpu.VMEM((2, KEYS, LIST * HEAD + ROW_EXTRA), jnp.bfloat16),
                pltpu.VMEM((2, n_seq, tokens, LIST * HEAD + ROW_EXTRA), jnp.bfloat16),
                pltpu.SMEM((1,), jnp.int32),
                pltpu.SMEM((1,), jnp.int32),
                pltpu.SemaphoreType.DMA((7,)),
                pltpu.SemaphoreType.DMA((7,)),
                pltpu.SemaphoreType.DMA((2,)),
                pltpu.SemaphoreType.DMA((slots,)),
                pltpu.SemaphoreType.DMA((slots,)),
                pltpu.SemaphoreType.DMA((2,)),
            ],
            compiler_params=pltpu.CompilerParams(
                collective_id=0, has_side_effects=True, vmem_limit_bytes=32 * 1024 * 1024
            ),
        )(queries, key_value_pairs, span_index, valid_count)

    return jax.shard_map(
        shards,
        mesh=mesh,
        in_specs=(P("span", "seq", None), P("span", "seq", None), P("span"), P("span")),
        out_specs=P("span", "seq", None),
        check_vma=False,
    )
```

time: 60.1 us -> 54.8 us (0.912)
  Pallas kernels: 56.2 us -> 50.9 us
    pallas_call x1, Pallas kernels: 56.2 us -> 50.9 us  [shards(): pl.pallas_call(functools.partial(kernel, n_span, n_seq), out_shape=jax.Sh...]
where the time goes in v2:
time: 54.8 us; the launch traced here: 54.6 us
  Pallas kernels  50.9 us (93%)
  local copies, waits for them, and re-layouts  2.37 us (4%)
  between operations  1.31 us (2%)
    pallas_call x1, Pallas kernels, shards(): pl.pallas_call(functools.partial(kernel, n_span, n_seq), out_shape=jax.Sh...  50.9 us
    unnamed x5, local copies, waits for them, and re-layouts  2.37 us

profile of v2, /device:TPU:1, one launch (start us, length us, event | category | flops | bytes accessed | tf_op | source)
XLA Modules:
  0.0 54.6 jit_solution(4585799895202609604)
XLA Ops:
  1.3 0.0 copy-start
  1.3 0.9 %copy-done = bf16[1,16,3072]{2,1,0:T(8,128)(2,1)S(1)} copy-done((bf16[1,16,3072]{2,1,0:T(8,128)(2,1)S(1)}, bf16[1,16,3072]{2,1,0:T(8,128)(2,1)}, u32[]{:S(2)}) %copy-start) | copy-done | bytes 98328
  2.2 0.0 copy-start.1
  2.2 0.8 %copy-done.1 = bf16[1,16,2048]{2,1,0:T(8,128)(2,1)S(1)} copy-done((bf16[1,16,2048]{2,1,0:T(8,128)(2,1)S(1)}, bf16[1,16,2048]{2,1,0:T(8,128)(2,1)}, u32[]{:S(2)}) %copy-start.1) | copy-done | bytes 65560
  3.0 50.9 %shard_map.46 = bf16[1,16,3072]{2,1,0:T(8,128)(2,1)S(1)} custom-call(bf16[1,16,3072]{2,1,0:T(8,128)(2,1)S(1)} %copy-done, bf16[1,16,2048]{2,1,0:T(8,128)(2,1)S(1)} %copy-done.1, s32[1]{0:T(128)S(6)} %copy.6.index_hbm, s32[1]{0:T(128)S(6)} %copy.7.count_hbm), custom_call_target="tpu_custom_call" | custom-call | tf_op jit(solution)/shard_map/pallas_call | solution.py:299
  54.0 0.6 %copy.8 = bf16[1,16,3072]{2,1,0:T(8,128)(2,1)} copy(bf16[1,16,3072]{2,1,0:T(8,128)(2,1)S(1)} %shard_map.46) | data formatting | bytes 196608
Async XLA Ops:
  1.3 0.9 %copy-start = (bf16[1,16,3072]{2,1,0:T(8,128)(2,1)S(1)}, bf16[1,16,3072]{2,1,0:T(8,128)(2,1)}, u32[]{:S(2)}) copy-start(bf16[1,16,3072]{2,1,0:T(8,128)(2,1)} %q_hbm.1) | copy-start | bytes 294916
  2.2 0.8 %copy-start.1 = (bf16[1,16,2048]{2,1,0:T(8,128)(2,1)S(1)}, bf16[1,16,2048]{2,1,0:T(8,128)(2,1)}, u32[]{:S(2)}) copy-start(bf16[1,16,2048]{2,1,0:T(8,128)(2,1)} %kv_hbm.1) | copy-start | bytes 196612

commit v3 on v2

--- a/solution.py
+++ b/solution.py
@@ -21,25 +21,25 @@
 
 
 TREES = (
-    {-7: -6, -6: -5, -5: -1, -4: -5, -3: -2, -2: -1, -1: 0, 1: 0, 2: 0, 3: 2, 4: 1, 5: 4, 6: 4, 7: 5, 8: -6},
-    {-7: -6, -6: -4, -5: -4, -4: 0, -3: -4, -2: -3, -1: 0, 1: 2, 2: 0, 3: 0, 4: 3, 5: 4, 6: 3, 7: 6, 8: -5},
+    {-7: -6, -6: -4, -5: -4, -4: -1, -3: -4, -2: -1, -1: 0, 1: 0, 2: 1, 3: 1, 4: 2, 5: 4, 6: 5, 7: 4, 8: -6},
+    {-7: -6, -6: -3, -5: -4, -4: -3, -3: 0, -2: -3, -1: 0, 1: 0, 2: 1, 3: 2, 4: 0, 5: 4, 6: 5, 7: 6, 8: -6},
 )
-GROUPS = ((0, -1), (2, 3), (-5, 4), (1, -3), (-6, -4), (-2, 6), (5, -7), (8, 7))
+GROUPS = ((0, 1), (-1, 2), (-2, -4), (4, 3), (-3, -6), (-5, 5), (-7, 7), (8, 6))
 EVENTS = (
-    ((0, -1), (0, 1), (1, -1), (0, 2),),
+    ((0, 1), (0, -1), (1, 1), (1, -1),),
+    ((1, -3),),
+    ((1, 4), (0, 2), (0, -2), (1, 2), (0, -4), (0, 3), (1, -2),),
+    ((1, -4),),
+    ((1, 5), (1, -6),),
     (),
-    ((1, -4), (1, 2), (1, 3), (0, -2), (0, 4), (0, -5), (0, 3), (1, -5), (1, -3), (1, 4), (1, 1),),
+    ((0, 4), (1, 3), (0, -5), (0, -3), (0, -6), (1, 6),),
+    ((1, -5),),
+    ((1, -7),),
     (),
-    ((1, -6), (0, -3),),
+    ((0, 5), (1, 8),),
+    ((0, -7),),
+    ((0, 7), (1, 7), (0, 8), (0, 6),),
     (),
-    ((0, 5), (0, -6), (1, 6),),
-    (),
-    ((0, -4), (1, 8), (1, -2), (1, -7), (0, 6),),
-    ((1, 5),),
-    ((0, -7),),
-    ((1, 7),),
-    ((0, 8),),
-    ((0, 7),),
     (),
 )
 CHILDREN = tuple(
@@ -321,7 +321,7 @@
                 pltpu.SemaphoreType.DMA((2,)),
             ],
             compiler_params=pltpu.CompilerParams(
-                collective_id=0, has_side_effects=True, vmem_limit_bytes=32 * 1024 * 1024
+                collective_id=0, has_side_effects=True, vmem_limit_bytes=60 * 1024 * 1024
             ),
         )(queries, key_value_pairs, span_index, valid_count)
 

time: 54.8 us -> 53.7 us (0.980)
  local copies, waits for them, and re-layouts: 2.37 us -> 1.54 us
    unnamed x5 -> x1, local copies, waits for them, and re-layouts: 2.37 us -> 1.54 us
where the time goes in v3:
time: 53.7 us; the launch traced here: 53.6 us
  Pallas kernels  50.7 us (94%)
  local copies, waits for them, and re-layouts  1.54 us (3%)
  between operations  1.3 us (2%)
    pallas_call x1, Pallas kernels, shards(): pl.pallas_call(functools.partial(kernel, n_span, n_seq), out_shape=jax.Sh...  50.7 us
    unnamed x1, local copies, waits for them, and re-layouts  1.54 us

profile of v3, /device:TPU:1, one launch (start us, length us, event | category | flops | bytes accessed | tf_op | source)
XLA Modules:
  0.0 53.6 jit_solution(7174174705481598086)
XLA Ops:
  1.3 50.7 %shard_map.46 = bf16[1,16,3072]{2,1,0:T(8,128)(2,1)} custom-call(bf16[1,16,3072]{2,1,0:T(8,128)(2,1)} %q_hbm.1, bf16[1,16,2048]{2,1,0:T(8,128)(2,1)} %kv_hbm.1, s32[1]{0:T(128)S(6)} %copy.6.index_hbm, s32[1]{0:T(128)S(6)} %copy.7.count_hbm), custom_call_target="tpu_custom_call" | custom-call | tf_op jit(solution)/shard_map/pallas_call | solution.py:299
  52.0 1.5 %copy.8 = bf16[1,16,3072]{2,1,0:T(8,128)(2,1)} copy(bf16[1,16,3072]{2,1,0:T(8,128)(2,1)} %shard_map.46) | data formatting | bytes 196608

commit v4 on v2

--- a/solution.py
+++ b/solution.py
@@ -21,29 +21,30 @@
 
 
 TREES = (
-    {-7: -6, -6: -5, -5: -1, -4: -5, -3: -2, -2: -1, -1: 0, 1: 0, 2: 0, 3: 2, 4: 1, 5: 4, 6: 4, 7: 5, 8: -6},
-    {-7: -6, -6: -4, -5: -4, -4: 0, -3: -4, -2: -3, -1: 0, 1: 2, 2: 0, 3: 0, 4: 3, 5: 4, 6: 3, 7: 6, 8: -5},
+    {-7: -6, -6: -4, -5: -4, -4: -3, -3: -2, -2: -1, -1: 0, 1: 0, 2: 1, 3: 2, 4: 3, 5: 3, 6: 5, 7: 4, 8: 7},
+    {-7: -6, -6: -3, -5: -4, -4: -3, -3: -2, -2: 0, -1: 0, 1: 0, 2: 1, 3: 4, 4: 0, 5: 4, 6: 5, 7: 5, 8: -6},
 )
-GROUPS = ((0, -1), (2, 3), (-5, 4), (1, -3), (-6, -4), (-2, 6), (5, -7), (8, 7))
+DIRECT = (3, -3)
+GROUPS = ((0, -1), (1, 3), (-3, -2), (4, -4), (2, 5), (-6, -5), (6, 7), (-7, 8))
 EVENTS = (
-    ((0, -1), (0, 1), (1, -1), (0, 2),),
-    (),
-    ((1, -4), (1, 2), (1, 3), (0, -2), (0, 4), (0, -5), (0, 3), (1, -5), (1, -3), (1, 4), (1, 1),),
-    (),
-    ((1, -6), (0, -3),),
-    (),
-    ((0, 5), (0, -6), (1, 6),),
-    (),
-    ((0, -4), (1, 8), (1, -2), (1, -7), (0, 6),),
-    ((1, 5),),
-    ((0, -7),),
-    ((1, 7),),
-    ((0, 8),),
-    ((0, 7),),
+    ((0, -1), (0, 1), (0, 3), (0, -3), (1, -1), (1, 1), (1, 3), (1, -3), (1, -2),),
+    (),
+    ((0, -2),),
+    ((1, 4),),
+    ((0, -4), (0, 2), (0, 4),),
+    (),
+    ((1, -4), (1, 2), (0, 5),),
+    ((1, -6), (1, 5),),
+    ((0, -5),),
+    ((0, -6),),
+    ((0, 7), (1, -5), (0, 6), (1, -7), (1, 6),),
+    (),
+    ((1, 8), (1, 7), (0, -7), (0, 8),),
+    (),
     (),
 )
 CHILDREN = tuple(
-    {parent: [child for child in tree if tree[child] == parent] for parent in set(tree.values())} for tree in TREES
+    {parent: [child for child in tree if tree[child] == parent and child not in DIRECT] for parent in set(tree.values())} for tree in TREES
 )
 
 
@@ -53,9 +54,9 @@
 
 def kernel(
     n_span, n_seq,
-    q_hbm, kv_hbm, index_hbm, count_hbm, out_ref,
-    kbuf, vbuf, qbuf, place_buf, max_ref, sum_ref, acc_ref, part_buf, got_buf, index_smem, count_smem,
-    a2a_send, a2a_recv, ring_send, k_recv, v_recv, int_sem,
+    q_hbm, kv_hbm, index_ref, count_ref, out_ref,
+    kbuf, vbuf, qbuf, place_buf, max_ref, sum_ref, acc_ref, part_buf, got_buf,
+    a2a_send, a2a_recv, ring_send, k_recv, v_recv,
 ):
     tokens = q_hbm.shape[1]
     half_spans = n_span // 2
@@ -77,33 +78,25 @@
         return (half * half_spans + z_at(offset) * 2 + core, seq)
 
     barrier = pltpu.get_barrier_semaphore()
-    for d in range(1, n_seq):
-        pl.semaphore_signal(barrier, inc=1, device_id=(span, seq ^ d), device_id_type=MESH)
-    for d in range(n_seq):
-        pl.semaphore_signal(barrier, inc=1, device_id=(partner_span, seq ^ d), device_id_type=MESH)
-    steps = sorted({abs(hops(child, parent)) for tree in TREES for child, parent in tree.items()})
-    for s in steps:
-        for device in (along(s), along(-s)):
-            pl.semaphore_signal(barrier, inc=1, device_id=device, device_id_type=MESH)
-    pl.semaphore_signal(barrier, inc=1, device_id=sibling, device_id_type=MESH)
-
-    ints = [
-        pltpu.make_async_copy(index_hbm, index_smem, int_sem.at[0]),
-        pltpu.make_async_copy(count_hbm, count_smem, int_sem.at[1]),
-    ]
-    for copy in ints:
-        copy.start()
+    peers = [(span, seq ^ d) for d in range(1, n_seq)]
+    peers += [(partner_span, seq ^ d) for d in range(n_seq)]
+    steps = sorted({child - parent for tree in TREES for child, parent in tree.items()} | {abs(n) for n in DIRECT})
+    steps = [s for s in steps if s > 0]
+    peers += [along(sign * s) for s in steps for sign in (1, -1)]
+    peers += [(along(n)[0], seq ^ d) for n in DIRECT for d in range(1, n_seq)]
+    peers.append(sibling)
+    for device in peers:
+        pl.semaphore_signal(barrier, inc=1, device_id=device, device_id_type=MESH)
+
     max_ref[...] = jnp.full(max_ref.shape, NO_MAX, jnp.float32)
     sum_ref[...] = jnp.zeros(sum_ref.shape, jnp.float32)
     acc_ref[...] = jnp.zeros(acc_ref.shape, jnp.float32)
-    for copy in ints:
-        copy.wait()
-    index = index_smem[0].astype(jnp.float32)
+    index = index_ref[0].astype(jnp.float32)
     lane = lax.broadcasted_iota(jnp.int32, (META, 128), 1)
-    kbuf[slot, KEYS:, :] = jnp.where(lane < count_smem[0], index, FAR).astype(jnp.bfloat16)
+    kbuf[slot, KEYS:, :] = jnp.where(lane < count_ref[0], index, FAR).astype(jnp.bfloat16)
     place_buf[0] = jnp.full((META, 128), index, jnp.float32).astype(jnp.bfloat16)
 
-    pl.semaphore_wait(barrier, 2 * n_seq + 2 * len(steps))
+    pl.semaphore_wait(barrier, len(peers))
 
     def send(src, dst, send_sem, recv_sem, device):
         pltpu.make_async_remote_copy(
@@ -118,15 +111,21 @@
     def columns(start, size):
         return pl.ds(pl.multiple_of(start, 128), size)
 
-    for part, buf in ((0, kbuf), (1, vbuf)):
-        for d in range(n_seq):
-            their = (seq ^ d) ^ half
-            src = kv_hbm.at[0, :, columns(their * 256 + part * 128, 128)]
-            dst = buf.at[slot, rows, :]
-            if d == 0:
-                pltpu.make_async_copy(src, dst, a2a_recv.at[part]).start()
-            else:
-                send(src, dst, a2a_send.at[part], a2a_recv.at[part], (span, seq ^ d))
+    meta = kbuf.at[slot, pl.ds(KEYS, META), :]
+    for n in DIRECT:
+        send(meta, meta, a2a_send.at[7], k_recv.at[slot], along(n))
+    for part, buf, recv in ((0, kbuf, k_recv), (1, vbuf, v_recv)):
+        for n in (*DIRECT, 0):
+            for d in range(n_seq):
+                their = (seq ^ d) ^ half
+                src = kv_hbm.at[0, :, columns(their * 256 + part * 128, 128)]
+                dst = buf.at[slot, rows, :]
+                if n:
+                    send(src, dst, a2a_send.at[8 + part], recv.at[slot], (along(n)[0], seq ^ d))
+                elif d:
+                    send(src, dst, a2a_send.at[part], a2a_recv.at[part], (span, seq ^ d))
+                else:
+                    pltpu.make_async_copy(src, dst, a2a_recv.at[part]).start()
 
     for d in range(n_seq):
         their = (seq ^ d) ^ half
@@ -161,20 +160,16 @@
     hand_on(0, 0)
     wait(vbuf.at[slot], a2a_recv.at[1])
     hand_on(1, 0)
-    wait(qbuf.at[0], a2a_recv.at[2])
-    wait(qbuf.at[1], a2a_recv.at[3])
-    wait(place_buf.at[1], a2a_recv.at[4])
-
-    def attend(b, places):
+
+    def attend(b, pairs):
         mine = place_buf[b].astype(jnp.float32)[:1]
-        pairs = [pl.ds(place * 2, 2) for place in places]
-        metas = [kbuf[pair, KEYS:, :].astype(jnp.float32) for pair in pairs]
-        biases = [jnp.where(meta[i, :1] <= mine, 0.0, HIDDEN) for meta in metas for i in range(2)]
+        metas = [kbuf[which, KEYS:, :].astype(jnp.float32) for pair in pairs for which in pair]
+        biases = [jnp.where(meta[:1] <= mine, 0.0, HIDDEN) for meta in metas]
         products = []
         for head in range(LIST):
             query = qbuf[b, :, head * HEAD : (head + 1) * HEAD]
             for pair in pairs:
-                keys = kbuf[pair, :KEYS, :].reshape(2 * KEYS, HEAD)
+                keys = jnp.concatenate([kbuf[which, :KEYS, :] for which in pair], axis=0)
                 products.append(
                     lax.dot_general(query, keys, (((1,), (1,)), ((), ())), preferred_element_type=jnp.float32)
                 )
@@ -198,7 +193,7 @@
             alpha, raw = weights[head]
             total = acc_ref[tile] * alpha
             for i, pair in enumerate(pairs):
-                values = vbuf[pair].reshape(2 * KEYS, HEAD)
+                values = jnp.concatenate([vbuf[which] for which in pair], axis=0)
                 total += jnp.dot(
                     jnp.concatenate(raw[2 * i : 2 * i + 2], axis=1), values, preferred_element_type=jnp.float32
                 )
@@ -238,34 +233,58 @@
             places.append(z_at(-offset))
         return places
 
+    def arrive(events):
+        for chunk, offset in events:
+            wait_for(chunk, z_at(-offset) * 2 + core)
+            hand_on(chunk, offset)
+
+    def wait_other(places):
+        for place in places:
+            for chunk in range(2):
+                wait_for(chunk, place * 2 + 1 - core)
+
     def loop(i, carry):
-        for at, events in enumerate(EVENTS):
+        for at, events in enumerate(EVENTS[:-1]):
             if events:
 
                 @pl.when(i == at)
                 def _():
-                    for chunk, offset in events:
-                        wait_for(chunk, z_at(-offset) * 2 + core)
-                        hand_on(chunk, offset)
+                    arrive(events)
+
+        @pl.when(i == 0)
+        def _():
+            wait(qbuf.at[0], a2a_recv.at[2])
+            wait(qbuf.at[1], a2a_recv.at[3])
+            wait(place_buf.at[1], a2a_recv.at[4])
 
         places = places_of(lax.div(i, 2))
 
         @pl.when(lax.rem(i, 2) == 0)
         def _():
-            for place in places:
-                for chunk in range(2):
-                    wait_for(chunk, place * 2 + 1 - core)
-
-        attend(1 - lax.rem(i, 2), places)
+            wait_other(places)
+
+        attend(1 - lax.rem(i, 2), [[place * 2, place * 2 + 1] for place in places])
         return carry
 
-    lax.fori_loop(0, 2 * len(GROUPS) - 1, loop, 0)
+    lax.fori_loop(0, len(EVENTS) - 1, loop, 0)
+    arrive(EVENTS[-1])
+    places = [z_at(-offset) for offset in GROUPS[-1]]
+    own = [[place * 2 + core for place in places]]
+    others = [[place * 2 + 1 - core for place in places]]
+    attend(1, own)
+    attend(0, own)
+    wait_other(places)
+    attend(1, others)
     finish(1)
-    attend(0, [z_at(-offset) for offset in GROUPS[-1]])
+    attend(0, others)
     finish(0)
 
-    wait(kbuf.at[pl.ds(0, half_spans - 1)], ring_send.at[0])
-    wait(vbuf.at[pl.ds(0, half_spans - 1)], ring_send.at[1])
+    wait(kbuf.at[pl.ds(0, half_spans - 1 - len(DIRECT))], ring_send.at[0])
+    wait(vbuf.at[pl.ds(0, half_spans - 1 - len(DIRECT))], ring_send.at[1])
+    if DIRECT:
+        wait(place_buf.at[pl.ds(0, len(DIRECT))], a2a_send.at[7])
+        wait(vbuf.at[pl.ds(0, len(DIRECT))], a2a_send.at[8])
+        wait(vbuf.at[pl.ds(0, len(DIRECT))], a2a_send.at[9])
     wait(vbuf.at[0, pl.ds(0, (n_seq - 1) * tokens), :], a2a_send.at[0])
     wait(vbuf.at[0, pl.ds(0, (n_seq - 1) * tokens), :], a2a_send.at[1])
     wait(qbuf.at[0, pl.ds(0, (n_seq - 1) * tokens), :], a2a_send.at[2])
@@ -299,31 +318,33 @@
         return pl.pallas_call(
             functools.partial(kernel, n_span, n_seq),
             out_shape=jax.ShapeDtypeStruct(queries.shape, jnp.bfloat16),
-            in_specs=[pl.BlockSpec(memory_space=pl.ANY)] * 4,
+            in_specs=[pl.BlockSpec(memory_space=pl.ANY)] * 2 + [pl.BlockSpec(memory_space=pltpu.SMEM)] * 2,
             out_specs=pl.BlockSpec(memory_space=pltpu.VMEM),
             scratch_shapes=[
                 pltpu.VMEM((slots, KEYS + META, HEAD), jnp.bfloat16),
                 pltpu.VMEM((slots, KEYS, HEAD), jnp.bfloat16),
                 pltpu.VMEM((2, KEYS, LIST * HEAD), jnp.bfloat16),
-                pltpu.VMEM((2, META, 128), jnp.bfloat16),
+                pltpu.VMEM((8, META, 128), jnp.bfloat16),
                 pltpu.VMEM((2 * LIST, KEYS, HEAD), jnp.float32),
                 pltpu.VMEM((2 * LIST, KEYS, HEAD), jnp.float32),
                 pltpu.VMEM((2 * LIST, KEYS, HEAD), jnp.float32),
                 pltpu.VMEM((2, KEYS, LIST * HEAD + ROW_EXTRA), jnp.bfloat16),
                 pltpu.VMEM((2, n_seq, tokens, LIST * HEAD + ROW_EXTRA), jnp.bfloat16),
-                pltpu.SMEM((1,), jnp.int32),
-                pltpu.SMEM((1,), jnp.int32),
-                pltpu.SemaphoreType.DMA((7,)),
+                pltpu.SemaphoreType.DMA((10,)),
                 pltpu.SemaphoreType.DMA((7,)),
                 pltpu.SemaphoreType.DMA((2,)),
                 pltpu.SemaphoreType.DMA((slots,)),
                 pltpu.SemaphoreType.DMA((slots,)),
-                pltpu.SemaphoreType.DMA((2,)),
             ],
             compiler_params=pltpu.CompilerParams(
                 collective_id=0, has_side_effects=True, vmem_limit_bytes=32 * 1024 * 1024
             ),
-        )(queries, key_value_pairs, span_index, valid_count)
+        )(
+            pltpu.with_memory_space_constraint(queries, pltpu.HBM),
+            pltpu.with_memory_space_constraint(key_value_pairs, pltpu.HBM),
+            span_index,
+            valid_count,
+        )
 
     return jax.shard_map(
         shards,

time: 54.8 us -> 51.7 us (0.943)
  local copies, waits for them, and re-layouts: 2.37 us -> 0.64 us
  Pallas kernels: 50.9 us -> 49.6 us
    unnamed x5 -> x1, local copies, waits for them, and re-layouts: 2.37 us -> 0.64 us
    pallas_call x1, Pallas kernels: 50.9 us -> 49.6 us  [shards(): pl.pallas_call(functools.partial(kernel, n_span, n_seq), out_shape=jax.Sh...]
where the time goes in v4:
time: 51.7 us; the launch traced here: 51.6 us
  Pallas kernels  49.6 us (96%)
  between operations  1.3 us (3%)
  local copies, waits for them, and re-layouts  0.64 us (1%)
    pallas_call x1, Pallas kernels, shards(): pl.pallas_call(functools.partial(kernel, n_span, n_seq), out_shape=jax.Sh...  49.6 us

profile of v4, /device:TPU:1, one launch (start us, length us, event | category | flops | bytes accessed | tf_op | source)
XLA Modules:
  0.0 51.6 jit_solution(4783618804786946439)
XLA Ops:
  1.3 49.6 %shard_map.46 = bf16[1,16,3072]{2,1,0:T(8,128)(2,1)S(1)} custom-call(bf16[1,16,3072]{2,1,0:T(8,128)(2,1)} %q_hbm.1, bf16[1,16,2048]{2,1,0:T(8,128)(2,1)} %kv_hbm.1, s32[1]{0:T(128)S(6)} %copy.6.index_ref, s32[1]{0:T(128)S(6)} %copy.7.count_ref), custom_call_target="tpu_custom_call" | custom-call | tf_op jit(solution)/shard_map/pallas_call | solution.py:318
  50.9 0.6 %copy.8 = bf16[1,16,3072]{2,1,0:T(8,128)(2,1)} copy(bf16[1,16,3072]{2,1,0:T(8,128)(2,1)S(1)} %shard_map.46) | data formatting | bytes 196608

commit v5 on v4

--- a/solution.py
+++ b/solution.py
@@ -12,6 +12,7 @@
 HEAD = 128
 LIST = 3
 KEYS = 128
+HALF = KEYS // 2
 META = 16
 ROW_EXTRA = 128
 SCALE = HEAD ** (-0.5) / math.log(2.0)
@@ -55,8 +56,8 @@
 def kernel(
     n_span, n_seq,
     q_hbm, kv_hbm, index_ref, count_ref, out_ref,
-    kbuf, vbuf, qbuf, place_buf, max_ref, sum_ref, acc_ref, part_buf, got_buf,
-    a2a_send, a2a_recv, ring_send, k_recv, v_recv,
+    kvbuf, metabuf, qbuf, place_buf, max_ref, sum_ref, acc_ref, part_buf, got_buf,
+    a2a_send, a2a_recv, ring_send, chunk_recv, meta_recv,
 ):
     tokens = q_hbm.shape[1]
     half_spans = n_span // 2
@@ -92,8 +93,8 @@
     sum_ref[...] = jnp.zeros(sum_ref.shape, jnp.float32)
     acc_ref[...] = jnp.zeros(acc_ref.shape, jnp.float32)
     index = index_ref[0].astype(jnp.float32)
-    lane = lax.broadcasted_iota(jnp.int32, (META, 128), 1)
-    kbuf[slot, KEYS:, :] = jnp.where(lane < count_ref[0], index, FAR).astype(jnp.bfloat16)
+    lane = lax.broadcasted_iota(jnp.int32, (1, 128), 1)
+    metabuf[slot] = jnp.where(lane < count_ref[0], index, FAR)
     place_buf[0] = jnp.full((META, 128), index, jnp.float32).astype(jnp.bfloat16)
 
     pl.semaphore_wait(barrier, len(peers))
@@ -111,21 +112,20 @@
     def columns(start, size):
         return pl.ds(pl.multiple_of(start, 128), size)
 
-    meta = kbuf.at[slot, pl.ds(KEYS, META), :]
     for n in DIRECT:
-        send(meta, meta, a2a_send.at[7], k_recv.at[slot], along(n))
-    for part, buf, recv in ((0, kbuf, k_recv), (1, vbuf, v_recv)):
-        for n in (*DIRECT, 0):
-            for d in range(n_seq):
-                their = (seq ^ d) ^ half
-                src = kv_hbm.at[0, :, columns(their * 256 + part * 128, 128)]
-                dst = buf.at[slot, rows, :]
-                if n:
-                    send(src, dst, a2a_send.at[8 + part], recv.at[slot], (along(n)[0], seq ^ d))
-                elif d:
-                    send(src, dst, a2a_send.at[part], a2a_recv.at[part], (span, seq ^ d))
-                else:
-                    pltpu.make_async_copy(src, dst, a2a_recv.at[part]).start()
+        send(metabuf.at[slot], metabuf.at[slot], ring_send.at[2], meta_recv.at[slot], along(n))
+    own_chunk = lax.div(seq, n_seq // 2)
+    for n in (0, *DIRECT):
+        for d in range(n_seq):
+            their = (seq ^ d) ^ half
+            src = kv_hbm.at[0, :, columns(their * 256, 256)]
+            dst = kvbuf.at[slot, rows, :]
+            if n:
+                send(src, dst, a2a_send.at[1], chunk_recv.at[own_chunk, slot], (along(n)[0], seq ^ d))
+            elif d:
+                send(src, dst, a2a_send.at[0], a2a_recv.at[own_chunk], (span, seq ^ d))
+            else:
+                pltpu.make_async_copy(src, dst, a2a_recv.at[own_chunk]).start()
 
     for d in range(n_seq):
         their = (seq ^ d) ^ half
@@ -142,13 +142,19 @@
 
     send(place_buf.at[0], place_buf.at[1], a2a_send.at[4], a2a_recv.at[4], (partner_span, seq ^ 1))
 
-    bufs, recvs = (kbuf, vbuf), (k_recv, v_recv)
+    def chunk_of(chunk, which):
+        return kvbuf.at[which, pl.ds(chunk * HALF, HALF), :]
 
     def pass_on(chunk, which, device):
-        send(bufs[chunk].at[which], bufs[chunk].at[which], ring_send.at[chunk], recvs[chunk].at[which], device)
+        ref = chunk_of(chunk, which)
+        send(ref, ref, ring_send.at[chunk], chunk_recv.at[chunk, which], device)
+        if chunk == 0:
+            send(metabuf.at[which], metabuf.at[which], ring_send.at[2], meta_recv.at[which], device)
 
     def wait_for(chunk, which):
-        wait(bufs[chunk].at[which], recvs[chunk].at[which])
+        if chunk == 0:
+            wait(metabuf.at[which], meta_recv.at[which])
+        wait(chunk_of(chunk, which), chunk_recv.at[chunk, which])
 
     def hand_on(chunk, offset):
         which = z_at(-offset) * 2 + core
@@ -156,20 +162,19 @@
             pass_on(chunk, which, along(hops(child, offset)))
         pass_on(chunk, which, sibling)
 
-    wait(kbuf.at[slot, pl.ds(0, KEYS), :], a2a_recv.at[0])
-    hand_on(0, 0)
-    wait(vbuf.at[slot], a2a_recv.at[1])
-    hand_on(1, 0)
+    for chunk in range(2):
+        wait(chunk_of(chunk, slot), a2a_recv.at[chunk])
+        hand_on(chunk, 0)
 
     def attend(b, pairs):
         mine = place_buf[b].astype(jnp.float32)[:1]
-        metas = [kbuf[which, KEYS:, :].astype(jnp.float32) for pair in pairs for which in pair]
-        biases = [jnp.where(meta[:1] <= mine, 0.0, HIDDEN) for meta in metas]
+        metas = [metabuf[which] for pair in pairs for which in pair]
+        biases = [jnp.where(meta <= mine, 0.0, HIDDEN) for meta in metas]
         products = []
         for head in range(LIST):
             query = qbuf[b, :, head * HEAD : (head + 1) * HEAD]
             for pair in pairs:
-                keys = jnp.concatenate([kbuf[which, :KEYS, :] for which in pair], axis=0)
+                keys = jnp.concatenate([kvbuf[which, :, :HEAD] for which in pair], axis=0)
                 products.append(
                     lax.dot_general(query, keys, (((1,), (1,)), ((), ())), preferred_element_type=jnp.float32)
                 )
@@ -193,7 +198,7 @@
             alpha, raw = weights[head]
             total = acc_ref[tile] * alpha
             for i, pair in enumerate(pairs):
-                values = jnp.concatenate([vbuf[which] for which in pair], axis=0)
+                values = jnp.concatenate([kvbuf[which, :, HEAD:] for which in pair], axis=0)
                 total += jnp.dot(
                     jnp.concatenate(raw[2 * i : 2 * i + 2], axis=1), values, preferred_element_type=jnp.float32
                 )
@@ -279,14 +284,12 @@
     attend(0, others)
     finish(0)
 
-    wait(kbuf.at[pl.ds(0, half_spans - 1 - len(DIRECT))], ring_send.at[0])
-    wait(vbuf.at[pl.ds(0, half_spans - 1 - len(DIRECT))], ring_send.at[1])
+    for chunk in range(2):
+        wait(kvbuf.at[pl.ds(0, half_spans - 1 - len(DIRECT)), pl.ds(0, HALF), :], ring_send.at[chunk])
+    wait(metabuf.at[pl.ds(0, half_spans - 1)], ring_send.at[2])
+    wait(kvbuf.at[0, pl.ds(0, (n_seq - 1) * tokens), :], a2a_send.at[0])
     if DIRECT:
-        wait(place_buf.at[pl.ds(0, len(DIRECT))], a2a_send.at[7])
-        wait(vbuf.at[pl.ds(0, len(DIRECT))], a2a_send.at[8])
-        wait(vbuf.at[pl.ds(0, len(DIRECT))], a2a_send.at[9])
-    wait(vbuf.at[0, pl.ds(0, (n_seq - 1) * tokens), :], a2a_send.at[0])
-    wait(vbuf.at[0, pl.ds(0, (n_seq - 1) * tokens), :], a2a_send.at[1])
+        wait(kvbuf.at[pl.ds(0, len(DIRECT))], a2a_send.at[1])
     wait(qbuf.at[0, pl.ds(0, (n_seq - 1) * tokens), :], a2a_send.at[2])
     wait(qbuf.at[1], a2a_send.at[3])
     wait(place_buf.at[0], a2a_send.at[4])
@@ -321,19 +324,19 @@
             in_specs=[pl.BlockSpec(memory_space=pl.ANY)] * 2 + [pl.BlockSpec(memory_space=pltpu.SMEM)] * 2,
             out_specs=pl.BlockSpec(memory_space=pltpu.VMEM),
             scratch_shapes=[
-                pltpu.VMEM((slots, KEYS + META, HEAD), jnp.bfloat16),
-                pltpu.VMEM((slots, KEYS, HEAD), jnp.bfloat16),
+                pltpu.VMEM((slots, KEYS, 2 * HEAD), jnp.bfloat16),
+                pltpu.VMEM((slots, 1, 128), jnp.float32),
                 pltpu.VMEM((2, KEYS, LIST * HEAD), jnp.bfloat16),
-                pltpu.VMEM((8, META, 128), jnp.bfloat16),
+                pltpu.VMEM((2, META, 128), jnp.bfloat16),
                 pltpu.VMEM((2 * LIST, KEYS, HEAD), jnp.float32),
                 pltpu.VMEM((2 * LIST, KEYS, HEAD), jnp.float32),
                 pltpu.VMEM((2 * LIST, KEYS, HEAD), jnp.float32),
                 pltpu.VMEM((2, KEYS, LIST * HEAD + ROW_EXTRA), jnp.bfloat16),
                 pltpu.VMEM((2, n_seq, tokens, LIST * HEAD + ROW_EXTRA), jnp.bfloat16),
-                pltpu.SemaphoreType.DMA((10,)),
                 pltpu.SemaphoreType.DMA((7,)),
-                pltpu.SemaphoreType.DMA((2,)),
-                pltpu.SemaphoreType.DMA((slots,)),
+                pltpu.SemaphoreType.DMA((7,)),
+                pltpu.SemaphoreType.DMA((3,)),
+                pltpu.SemaphoreType.DMA((2, slots)),
                 pltpu.SemaphoreType.DMA((slots,)),
             ],
             compiler_params=pltpu.CompilerParams(

time: 51.7 us -> 51.9 us (level)
  no operation moved by 1% of the time
where the time goes in v5:
time: 51.9 us; the launch traced here: 51.8 us
  Pallas kernels  49.8 us (96%)
  between operations  1.3 us (3%)
  local copies, waits for them, and re-layouts  0.64 us (1%)
    pallas_call x1, Pallas kernels, shards(): pl.pallas_call(functools.partial(kernel, n_span, n_seq), out_shape=jax.Sh...  49.8 us

profile of v5, /device:TPU:1, one launch (start us, length us, event | category | flops | bytes accessed | tf_op | source)
XLA Modules:
  0.0 51.8 jit_solution(8845852967207064596)
XLA Ops:
  1.3 49.8 %shard_map.46 = bf16[1,16,3072]{2,1,0:T(8,128)(2,1)S(1)} custom-call(bf16[1,16,3072]{2,1,0:T(8,128)(2,1)} %q_hbm.1, bf16[1,16,2048]{2,1,0:T(8,128)(2,1)} %kv_hbm.1, s32[1]{0:T(128)S(6)} %copy.6.index_ref, s32[1]{0:T(128)S(6)} %copy.7.count_ref), custom_call_target="tpu_custom_call" | custom-call | tf_op jit(solution)/shard_map/pallas_call | solution.py:321
  51.1 0.6 %copy.8 = bf16[1,16,3072]{2,1,0:T(8,128)(2,1)} copy(bf16[1,16,3072]{2,1,0:T(8,128)(2,1)S(1)} %shard_map.46) | data formatting | bytes 196608

commit v6 on v5

--- a/solution.py
+++ b/solution.py
@@ -22,25 +22,25 @@
 
 
 TREES = (
-    {-7: -6, -6: -4, -5: -4, -4: -3, -3: -2, -2: -1, -1: 0, 1: 0, 2: 1, 3: 2, 4: 3, 5: 3, 6: 5, 7: 4, 8: 7},
-    {-7: -6, -6: -3, -5: -4, -4: -3, -3: -2, -2: 0, -1: 0, 1: 0, 2: 1, 3: 4, 4: 0, 5: 4, 6: 5, 7: 5, 8: -6},
+    {-7: -4, -6: -5, -5: -4, -4: -1, -3: -4, -2: -1, -1: 3, 1: -2, 2: 1, 3: 0, 4: 3, 5: 3, 6: 5, 7: 5, 8: -7},
+    {-7: -6, -6: -3, -5: -6, -4: -3, -3: 0, -2: -3, -1: 2, 1: -3, 2: 1, 3: 2, 4: 1, 5: 4, 6: 4, 7: 6, 8: -6},
 )
-DIRECT = (3, -3)
-GROUPS = ((0, -1), (1, 3), (-3, -2), (4, -4), (2, 5), (-6, -5), (6, 7), (-7, 8))
+DIRECT = (1, -1)
+GROUPS = ((0, 1), (-1, 2), (-4, 4), (-2, 3), (-3, 5), (-7, -5), (6, -6), (8, 7))
 EVENTS = (
-    ((0, -1), (0, 1), (0, 3), (0, -3), (1, -1), (1, 1), (1, 3), (1, -3), (1, -2),),
-    (),
-    ((0, -2),),
-    ((1, 4),),
-    ((0, -4), (0, 2), (0, 4),),
-    (),
-    ((1, -4), (1, 2), (0, 5),),
-    ((1, -6), (1, 5),),
-    ((0, -5),),
-    ((0, -6),),
-    ((0, 7), (1, -5), (0, 6), (1, -7), (1, 6),),
-    (),
-    ((1, 8), (1, 7), (0, -7), (0, 8),),
+    ((0, 1), (0, -1), (1, 1), (1, -1), (0, 3), (1, -3), (0, 2),),
+    (),
+    ((0, -2), (1, 2), (0, -4), (1, 4), (1, -4), (0, 4),),
+    ((1, -2),),
+    ((1, -6), (0, 5), (1, 3), (0, -3), (0, -5),),
+    (),
+    ((1, 5), (0, -7), (1, 6), (1, -7),),
+    ((1, -5),),
+    ((0, 6), (1, 8), (0, -6),),
+    ((0, 7),),
+    ((0, 8), (1, 7),),
+    (),
+    (),
     (),
     (),
 )
@@ -89,9 +89,6 @@
     for device in peers:
         pl.semaphore_signal(barrier, inc=1, device_id=device, device_id_type=MESH)
 
-    max_ref[...] = jnp.full(max_ref.shape, NO_MAX, jnp.float32)
-    sum_ref[...] = jnp.zeros(sum_ref.shape, jnp.float32)
-    acc_ref[...] = jnp.zeros(acc_ref.shape, jnp.float32)
     index = index_ref[0].astype(jnp.float32)
     lane = lax.broadcasted_iota(jnp.int32, (1, 128), 1)
     metabuf[slot] = jnp.where(lane < count_ref[0], index, FAR)
@@ -141,6 +138,10 @@
         send(src, qbuf.at[1, rows, :], a2a_send.at[3], a2a_recv.at[3], (partner_span, seq ^ d))
 
     send(place_buf.at[0], place_buf.at[1], a2a_send.at[4], a2a_recv.at[4], (partner_span, seq ^ 1))
+
+    max_ref[...] = jnp.full(max_ref.shape, NO_MAX, jnp.float32)
+    sum_ref[...] = jnp.zeros(sum_ref.shape, jnp.float32)
+    acc_ref[...] = jnp.zeros(acc_ref.shape, jnp.float32)
 
     def chunk_of(chunk, which):
         return kvbuf.at[which, pl.ds(chunk * HALF, HALF), :]

time: 51.9 us -> 50.1 us (0.965); the launches traced: 51.8 us -> 49.3 us
  Pallas kernels: 49.8 us -> 47.4 us
    pallas_call x1, Pallas kernels: 49.8 us -> 47.4 us  [shards(): pl.pallas_call(functools.partial(kernel, n_span, n_seq), out_shape=jax.Sh...]
where the time goes in v6:
time: 50.1 us; the launch traced here: 49.3 us
  Pallas kernels  47.4 us (95%)
  between operations  1.3 us (3%)
  local copies, waits for them, and re-layouts  0.64 us (1%)
    pallas_call x1, Pallas kernels, shards(): pl.pallas_call(functools.partial(kernel, n_span, n_seq), out_shape=jax.Sh...  47.4 us

profile of v6, /device:TPU:1, one launch (start us, length us, event | category | flops | bytes accessed | tf_op | source)
XLA Modules:
  0.0 49.3 jit_solution(1901521366556502290)
XLA Ops:
  1.3 47.4 %shard_map.46 = bf16[1,16,3072]{2,1,0:T(8,128)(2,1)S(1)} custom-call(bf16[1,16,3072]{2,1,0:T(8,128)(2,1)} %q_hbm.1, bf16[1,16,2048]{2,1,0:T(8,128)(2,1)} %kv_hbm.1, s32[1]{0:T(128)S(6)} %copy.6.index_ref, s32[1]{0:T(128)S(6)} %copy.7.count_ref), custom_call_target="tpu_custom_call" | custom-call | tf_op jit(solution)/shard_map/pallas_call | solution.py:322
  48.7 0.6 %copy.8 = bf16[1,16,3072]{2,1,0:T(8,128)(2,1)} copy(bf16[1,16,3072]{2,1,0:T(8,128)(2,1)S(1)} %shard_map.46) | data formatting | bytes 196608

commit v7 on v6

--- a/solution.py
+++ b/solution.py
@@ -72,6 +72,8 @@
     partner_span = (1 - half) * half_spans + slot
     sibling = (half * half_spans + z * 2 + (1 - core), seq)
 
+    far_first = sorted(range(n_seq), key=lambda d: -(d // 2 == 2) * 4 - d % 2 - (d > 1) * 2)
+
     def z_at(offset):
         return lax.rem(z + offset + n_z, n_z)
 
@@ -113,7 +115,7 @@
         send(metabuf.at[slot], metabuf.at[slot], ring_send.at[2], meta_recv.at[slot], along(n))
     own_chunk = lax.div(seq, n_seq // 2)
     for n in (0, *DIRECT):
-        for d in range(n_seq):
+        for d in far_first:
             their = (seq ^ d) ^ half
             src = kv_hbm.at[0, :, columns(their * 256, 256)]
             dst = kvbuf.at[slot, rows, :]
@@ -220,7 +222,7 @@
             stats = jnp.where(lane == 3 * head + 2, total - high, stats)
             part_buf[b, :, head * HEAD : (head + 1) * HEAD] = (acc_ref[tile] * factor).astype(jnp.bfloat16)
         part_buf[b, :, LIST * HEAD :] = stats.astype(jnp.bfloat16)
-        for d in range(n_seq):
+        for d in far_first:
             to = seq ^ d
             src = part_buf.at[b, pl.ds(pl.multiple_of(to * tokens, tokens), tokens), :]
             dst = got_buf.at[b, group]

time: 50.1 us -> 49.1 us (0.980)
  Pallas kernels: 47.4 us -> 46.5 us
    pallas_call x1, Pallas kernels: 47.4 us -> 46.5 us  [shards(): pl.pallas_call(functools.partial(kernel, n_span, n_seq), out_shape=jax.Sh...]
where the time goes in v7:
time: 49.1 us; the launch traced here: 48.4 us
  Pallas kernels  46.5 us (95%)
  between operations  1.3 us (3%)
  local copies, waits for them, and re-layouts  0.64 us (1%)
    pallas_call x1, Pallas kernels, shards(): pl.pallas_call(functools.partial(kernel, n_span, n_seq), out_shape=jax.Sh...  46.5 us

profile of v7, /device:TPU:1, one launch (start us, length us, event | category | flops | bytes accessed | tf_op | source)
XLA Modules:
  0.0 48.4 jit_solution(7111892426587082454)
XLA Ops:
  1.3 46.5 %shard_map.46 = bf16[1,16,3072]{2,1,0:T(8,128)(2,1)S(1)} custom-call(bf16[1,16,3072]{2,1,0:T(8,128)(2,1)} %q_hbm.1, bf16[1,16,2048]{2,1,0:T(8,128)(2,1)} %kv_hbm.1, s32[1]{0:T(128)S(6)} %copy.6.index_ref, s32[1]{0:T(128)S(6)} %copy.7.count_ref), custom_call_target="tpu_custom_call" | custom-call | tf_op jit(solution)/shard_map/pallas_call | solution.py:324
  47.8 0.6 %copy.8 = bf16[1,16,3072]{2,1,0:T(8,128)(2,1)} copy(bf16[1,16,3072]{2,1,0:T(8,128)(2,1)S(1)} %shard_map.46) | data formatting | bytes 196608

commit v8 on v7

--- a/solution.py
+++ b/solution.py
@@ -38,8 +38,8 @@
     ((1, -5),),
     ((0, 6), (1, 8), (0, -6),),
     ((0, 7),),
-    ((0, 8), (1, 7),),
-    (),
+    ((0, 8),),
+    ((1, 7),),
     (),
     (),
     (),
@@ -169,25 +169,25 @@
         wait(chunk_of(chunk, slot), a2a_recv.at[chunk])
         hand_on(chunk, 0)
 
-    def attend(b, pairs):
-        mine = place_buf[b].astype(jnp.float32)[:1]
+    def attend(spans, pairs):
         metas = [metabuf[which] for pair in pairs for which in pair]
-        biases = [jnp.where(meta <= mine, 0.0, HIDDEN) for meta in metas]
+        mine = [place_buf[b].astype(jnp.float32)[:1] for b in spans]
+        biases = [[jnp.where(meta <= own, 0.0, HIDDEN) for meta in metas] for own in mine]
+        work = [(i, b, head) for i, b in enumerate(spans) for head in range(LIST)]
+        keys = [jnp.concatenate([kvbuf[which, :, :HEAD] for which in pair], axis=0) for pair in pairs]
+        values = [jnp.concatenate([kvbuf[which, :, HEAD:] for which in pair], axis=0) for pair in pairs]
         products = []
-        for head in range(LIST):
+        for _, b, head in work:
             query = qbuf[b, :, head * HEAD : (head + 1) * HEAD]
-            for pair in pairs:
-                keys = jnp.concatenate([kvbuf[which, :, :HEAD] for which in pair], axis=0)
-                products.append(
-                    lax.dot_general(query, keys, (((1,), (1,)), ((), ())), preferred_element_type=jnp.float32)
-                )
+            products.append([
+                lax.dot_general(query, k, (((1,), (1,)), ((), ())), preferred_element_type=jnp.float32) for k in keys
+            ])
         weights = []
-        for head in range(LIST):
+        for (i, b, head), product in zip(work, products):
             tile = b * LIST + head
-            scores = []
-            for i, bias in enumerate(biases):
-                product = products[head * len(pairs) + i // 2]
-                scores.append(product[:, i % 2 * KEYS : (i % 2 + 1) * KEYS] * SCALE + bias)
+            scores = [
+                product[j // 2][:, j % 2 * KEYS : (j % 2 + 1) * KEYS] * SCALE + bias for j, bias in enumerate(biases[i])
+            ]
             old_max = max_ref[tile]
             top = functools.reduce(jnp.maximum, scores)
             new_max = jnp.maximum(old_max, jnp.max(top, axis=-1, keepdims=True))
@@ -196,14 +196,12 @@
             max_ref[tile] = new_max
             sum_ref[tile] = sum_ref[tile] * alpha + functools.reduce(jnp.add, raw)
             weights.append((alpha, [w.astype(jnp.bfloat16) for w in raw]))
-        for head in range(LIST):
+        for (_, b, head), (alpha, raw) in zip(work, weights):
             tile = b * LIST + head
-            alpha, raw = weights[head]
             total = acc_ref[tile] * alpha
-            for i, pair in enumerate(pairs):
-                values = jnp.concatenate([kvbuf[which, :, HEAD:] for which in pair], axis=0)
+            for j, v in enumerate(values):
                 total += jnp.dot(
-                    jnp.concatenate(raw[2 * i : 2 * i + 2], axis=1), values, preferred_element_type=jnp.float32
+                    jnp.concatenate(raw[2 * j : 2 * j + 2], axis=1), v, preferred_element_type=jnp.float32
                 )
             acc_ref[tile] = total
 
@@ -271,7 +269,7 @@
         def _():
             wait_other(places)
 
-        attend(1 - lax.rem(i, 2), [[place * 2, place * 2 + 1] for place in places])
+        attend([1 - lax.rem(i, 2)], [[place * 2, place * 2 + 1] for place in places])
         return carry
 
     lax.fori_loop(0, len(EVENTS) - 1, loop, 0)
@@ -279,12 +277,10 @@
     places = [z_at(-offset) for offset in GROUPS[-1]]
     own = [[place * 2 + core for place in places]]
     others = [[place * 2 + 1 - core for place in places]]
-    attend(1, own)
-    attend(0, own)
+    attend([1, 0], own)
     wait_other(places)
-    attend(1, others)
+    attend([1, 0], others)
     finish(1)
-    attend(0, others)
     finish(0)
 
     for chunk in range(2):
@@ -300,17 +296,17 @@
     wait(got_buf.at[1], a2a_recv.at[6])
     wait(got_buf.at[0], a2a_recv.at[5])
     for g in range(n_seq):
-        stats = [got_buf[b, g, :, LIST * HEAD :].astype(jnp.float32) for b in range(2)]
+        tops = [got_buf[b, g, :, LIST * HEAD :].astype(jnp.float32) for b in range(2)]
+        totals = [pltpu.roll(t, 127, 1) + pltpu.roll(t, 126, 1) for t in tops]
+        top = jnp.maximum(*tops)
+        shares = [jnp.exp2(t - top) for t in tops]
+        whole = shares[0] * totals[0] + shares[1] * totals[1]
+        shares = [s / whole for s in shares]
         for head in range(LIST):
-            tops = [s[:, 3 * head : 3 * head + 1] for s in stats]
-            totals = [s[:, 3 * head + 1 : 3 * head + 2] + s[:, 3 * head + 2 : 3 * head + 3] for s in stats]
-            top = jnp.maximum(*tops)
-            shares = [jnp.exp2(t - top) for t in tops]
-            whole = shares[0] * totals[0] + shares[1] * totals[1]
-            shares = [s / whole for s in shares]
+            mine = [s[:, 3 * head : 3 * head + 1] for s in shares]
             parts = [got_buf[b, g, :, head * HEAD : (head + 1) * HEAD].astype(jnp.float32) for b in range(2)]
             place = (g * LIST + head) * HEAD
-            out_ref[0, :, place : place + HEAD] = (parts[0] * shares[0] + parts[1] * shares[1]).astype(jnp.bfloat16)
+            out_ref[0, :, place : place + HEAD] = (parts[0] * mine[0] + parts[1] * mine[1]).astype(jnp.bfloat16)
     wait(part_buf.at[0, pl.ds(0, (n_seq - 1) * tokens), :], a2a_send.at[5])
     wait(part_buf.at[1], a2a_send.at[6])
 

time: 49.1 us -> 49.1 us (level)
  no operation moved by 1% of the time
where the time goes in v8:
time: 49.1 us; the launch traced here: 48.5 us
  Pallas kernels  46.5 us (95%)
  between operations  1.3 us (3%)
  local copies, waits for them, and re-layouts  0.64 us (1%)
    pallas_call x1, Pallas kernels, shards(): pl.pallas_call(functools.partial(kernel, n_span, n_seq), out_shape=jax.Sh...  46.5 us

profile of v8, /device:TPU:1, one launch (start us, length us, event | category | flops | bytes accessed | tf_op | source)
XLA Modules:
  0.0 48.5 jit_solution(7563734389510565463)
XLA Ops:
  1.3 46.5 %shard_map.46 = bf16[1,16,3072]{2,1,0:T(8,128)(2,1)S(1)} custom-call(bf16[1,16,3072]{2,1,0:T(8,128)(2,1)} %q_hbm.1, bf16[1,16,2048]{2,1,0:T(8,128)(2,1)} %kv_hbm.1, s32[1]{0:T(128)S(6)} %copy.6.index_ref, s32[1]{0:T(128)S(6)} %copy.7.count_ref), custom_call_target="tpu_custom_call" | custom-call | tf_op jit(solution)/shard_map/pallas_call | solution.py:320
  47.8 0.6 %copy.8 = bf16[1,16,3072]{2,1,0:T(8,128)(2,1)} copy(bf16[1,16,3072]{2,1,0:T(8,128)(2,1)S(1)} %shard_map.46) | data formatting | bytes 196608
